TPU v7x, 512 devices: a whole 4x4x16 slice. The times are simulated.
512 devices in a mesh: samp: 128 (over z, x, core), rep: 4 (over y).
Axes of the slice: x: 4, y: 4, z: 16, core: 2. Of those that a mesh axis runs over, the one named last changes fastest.
Arguments:
- read_blocks: bfloat16 [4, 512, 221, 8, 128], P('rep', 'samp'), may hold values from -6 to 6
- block_counts: int32 [4, 128], P('rep'), may hold values from 1 to 4, as said below
- block_reads: int32 [4, 512], P('rep'), may hold values from 32 to 128
- block_starts: int32 [4, 512], P('rep'), may hold values from 0 to 803
- conv_weight: bfloat16 [3, 8, 64], replicated, may hold values from -1.25 to 1.25
- conv_bias: float32 [64], replicated, may hold values from -3 to 3
- mix_weight: bfloat16 [64, 64], replicated, may hold values from -0.75 to 0.75
- pool_query: float32 [64], replicated, may hold values from -0.75 to 0.75
- site_cotangent: float32 [4, 128, 64, 1024], P('rep', 'samp'), may hold values from -2.5 to 2.5
Outputs:
- pooled_sites: float32 [4, 128, 64, 1024], P('rep', 'samp')
- grad_conv: float32 [3, 8, 64], replicated
- grad_bias: float32 [64], replicated
- grad_mix: float32 [64, 64], replicated
- grad_query: float32 [64], replicated
Inputs may be any that keep to these rules, and one draw needn't show every extreme that they name: `block_counts`: samples 2k and 2k + 1 of a window form a tumor and normal pair: one of them holds 2 to 4 blocks, the other 1 or 2, and the pair holds at most 6 blocks; in every window the first and the last pair hold 4 and 2 blocks; in the last pair the sample of even index holds the 4 in windows of even index, the sample of odd index in windows of odd index.
All inputs are finite; a program needn't handle non-finite values.
Results may differ from a plain program's by a relative error of at most 0.0034.
Values may be sent and summed in bfloat16 or wider, within the bound.
No kernel may reach another device: no remote copies, remote signals or barrier semaphores. Data moves between devices by JAX's collectives and lax.ppermute only.
A program may use at most 128 MiB of HBM per device.

v0:
```python
import jax
import jax.numpy as jnp
from jax import lax
from jax.sharding import PartitionSpec as P

CAP = 3
PACK = 2


def partner_2(value, axis, stride):
    mask = 2**stride
    pairs = [(source, source ^ mask) for source in range(lax.axis_size(axis))]
    return lax.ppermute(value, axis, pairs)


def make_taps(pileup):
    border = jnp.zeros_like(pileup[:1])
    padded = jnp.concatenate([border, pileup, border], axis=0)
    return jnp.stack([padded[:-2], padded[1:-1], padded[2:]], axis=1)


def pooling_terms(second_out, pool_query, live_mask):
    feature = jax.nn.silu(second_out)
    opening = jax.nn.sigmoid(jnp.sum(feature * pool_query[None, :, None], axis=1))
    return (feature, opening, opening * live_mask[None, :])


def first_layer(pileup, conv_weight, conv_bias):
    pre_relu = jnp.einsum(
        "ptcr,tcf->pfr", make_taps(pileup), conv_weight, preferred_element_type=jnp.float32
    )
    return jax.nn.relu(pre_relu + conv_bias[None, :, None]).astype(jnp.bfloat16)


def second_layer(hidden, mix_weight):
    return jnp.einsum("pgr,gf->pfr", hidden, mix_weight, preferred_element_type=jnp.float32)


def forward_slot(pileup, live_mask, conv_weight, conv_bias, mix_weight, pool_query):
    hidden = first_layer(pileup, conv_weight, conv_bias)
    second_out = second_layer(hidden, mix_weight)
    feature, opening, read_weight = pooling_terms(second_out, pool_query, live_mask)
    numerator = jnp.sum(feature * read_weight[:, None, :], axis=2).T
    denominator = jnp.sum(read_weight, axis=1)
    return (numerator, denominator, hidden, second_out)


def backward_slot(
    pileup, live_mask, hidden, second_out, mix_weight, pool_query, d_numerator, d_denominator
):
    feature, opening, read_weight = pooling_terms(second_out, pool_query, live_mask)
    d_weight = jnp.sum(feature * d_numerator.T[:, :, None], axis=1) + d_denominator[:, None]
    d_score = d_weight * live_mask[None, :] * opening * (1.0 - opening)
    d_feature = (
        d_numerator.T[:, :, None] * read_weight[:, None, :]
        + d_score[:, None, :] * pool_query[None, :, None]
    )
    g_query = jnp.sum(d_score[:, None, :] * feature, axis=(0, 2))
    sigmoid_out = jax.nn.sigmoid(second_out)
    d_second = (d_feature * sigmoid_out * (1.0 + second_out * (1.0 - sigmoid_out))).astype(
        jnp.bfloat16
    )
    g_mix = jnp.einsum("pgr,pfr->gf", hidden, d_second, preferred_element_type=jnp.float32)
    d_hidden = jnp.einsum("pfr,gf->pgr", d_second, mix_weight, preferred_element_type=jnp.float32)
    d_relu = jnp.where(hidden > 0, d_hidden, 0.0).astype(jnp.bfloat16)
    g_bias = jnp.sum(d_relu.astype(jnp.float32), axis=(0, 2))
    g_conv = jnp.einsum(
        "ptcr,pfr->tcf", make_taps(pileup), d_relu, preferred_element_type=jnp.float32
    )
    return (g_conv, g_bias, g_mix, g_query)


def place_window(numerator, denominator, start, site_total):
    anchor = jnp.zeros_like(start)
    num_win = lax.dynamic_update_slice(
        jnp.zeros((numerator.shape[0], site_total), jnp.float32), numerator, (anchor, start)
    )
    den_win = lax.dynamic_update_slice(jnp.zeros((site_total,), jnp.float32), denominator, (start,))
    return (num_win, den_win)


def cut_window(num_win, den_win, start, width):
    anchor = jnp.zeros_like(start)
    return (
        lax.dynamic_slice(num_win, (anchor, start), (num_win.shape[0], width)),
        lax.dynamic_slice(den_win, (start,), (width,)),
    )


def owner_step(site_num, site_den, cotangent):
    safe_den = jnp.maximum(site_den, 1.0)
    pooled = site_num / safe_den
    d_num = cotangent / safe_den
    d_den = jnp.where(
        site_den > 1.0, -jnp.sum(cotangent * site_num, axis=0) / (safe_den * safe_den), 0.0
    )
    return (pooled, d_num, d_den)


def run_forward(pileups, live_masks, weights):
    conv_weight, conv_bias, mix_weight, pool_query = weights

    def single(element):
        outcome = forward_slot(
            element[0], element[1], conv_weight, conv_bias, mix_weight, pool_query
        )
        return outcome[:3]

    return lax.map(single, (pileups, live_masks))


def run_backward(pileups, live_masks, saved, d_numerators, d_denominators, weights):
    conv_weight, conv_bias, mix_weight, pool_query = weights

    def single(running, element):
        pileup, live_mask, hidden, d_numerator, d_denominator = element
        second_out = second_layer(hidden, mix_weight)
        terms = backward_slot(
            pileup,
            live_mask,
            hidden,
            second_out,
            mix_weight,
            pool_query,
            d_numerator,
            d_denominator,
        )
        return (
            tuple((accumulated + increment for accumulated, increment in zip(running, terms))),
            None,
        )

    start_grads = (
        jnp.zeros(conv_weight.shape, jnp.float32),
        jnp.zeros(conv_bias.shape, jnp.float32),
        jnp.zeros(mix_weight.shape, jnp.float32),
        jnp.zeros(pool_query.shape, jnp.float32),
    )
    elements = (pileups, live_masks) + tuple(saved[2:]) + (d_numerators, d_denominators)
    gradients, _ = lax.scan(single, start_grads, elements)
    return gradients


def on_device(
    read_blocks,
    block_counts,
    block_reads,
    block_starts,
    conv_weight,
    conv_bias,
    mix_weight,
    pool_query,
    site_cotangent,
):
    slot_total = read_blocks.shape[1]
    positions = read_blocks.shape[2]
    read_total = read_blocks.shape[4]
    site_total = site_cotangent.shape[3]
    holdings = read_blocks[0]
    counts_all = block_counts[0]
    reads_all = block_reads[0]
    starts_all = block_starts[0]
    cotangent = site_cotangent[0, 0]
    weights = (conv_weight, conv_bias, mix_weight, pool_query)
    device_index = lax.axis_index("samp")
    read_index = jnp.arange(read_total, dtype=jnp.int32)

    def place_many(numerators, denominators, starts):
        placed = jax.vmap(
            lambda one_num, one_den, one_start: place_window(
                one_num, one_den, one_start, site_total
            )
        )(numerators, denominators, starts)
        return (jnp.sum(placed[0], axis=0), jnp.sum(placed[1], axis=0))

    def cut_many(num_win, den_win, starts):
        return jax.vmap(lambda one_start: cut_window(num_win, den_win, one_start, positions))(
            starts
        )

    member = device_index % 2
    partner = 1 - member
    pair_base = device_index - member
    first_count = counts_all[pair_base]
    pair_total = first_count + counts_all[pair_base + 1]
    my_first = member * first_count
    my_count = counts_all[device_index]
    send_order = jnp.maximum(CAP * partner, my_first) + jnp.arange(PACK, dtype=jnp.int32)
    send_slot = send_order - my_first
    send_active = (send_order < CAP * partner + CAP) & (send_slot < my_count)
    packet = jnp.where(
        send_active[:, None, None, None],
        jnp.take(holdings, jnp.clip(send_slot, 0, slot_total - 1), axis=0),
        jnp.zeros((), jnp.bfloat16),
    )
    arrived = partner_2(packet, "samp", 0)
    slot_order = CAP * member + jnp.arange(CAP, dtype=jnp.int32)
    slot_active = slot_order < pair_total
    source = (slot_order >= first_count).astype(jnp.int32)
    source_first = source * first_count
    slot_block = slot_order - source_first
    from_self = source == member
    home_pick = jnp.take(holdings, jnp.clip(slot_block, 0, slot_total - 1), axis=0)
    packet_slot = slot_order - jnp.maximum(CAP * member, source_first)
    away_pick = jnp.take(arrived, jnp.clip(packet_slot, 0, PACK - 1), axis=0)
    pileups = jnp.where(from_self[:, None, None, None], home_pick, away_pick)
    block_ids = (pair_base + source) * slot_total + jnp.clip(slot_block, 0, slot_total - 1)
    slot_reads = reads_all[block_ids]
    slot_starts = starts_all[block_ids]
    live_masks = ((read_index[None, :] < slot_reads[:, None]) & slot_active[:, None]).astype(
        jnp.float32
    )
    saved = run_forward(pileups, live_masks, weights)
    numerators, denominators = (saved[0], saved[1])
    self_mask = from_self.astype(jnp.float32)
    other_mask = 1.0 - self_mask
    home_num, home_den = place_many(
        numerators * self_mask[:, None, None], denominators * self_mask[:, None], slot_starts
    )
    away_num, away_den = place_many(
        numerators * other_mask[:, None, None], denominators * other_mask[:, None], slot_starts
    )
    got_num, got_den = partner_2((away_num, away_den), "samp", 0)
    pooled, d_num, d_den = owner_step(home_num + got_num, home_den + got_den, cotangent)
    far_num, far_den = partner_2((d_num, d_den), "samp", 0)
    home_cut = cut_many(d_num, d_den, slot_starts)
    away_cut = cut_many(far_num, far_den, slot_starts)
    d_numerators = jnp.where(from_self[:, None, None], home_cut[0], away_cut[0])
    d_denominators = jnp.where(from_self[:, None], home_cut[1], away_cut[1])
    gradients = run_backward(pileups, live_masks, saved, d_numerators, d_denominators, weights)
    totals = lax.psum((gradients[0], gradients[1], gradients[2], gradients[3]), ("samp", "rep"))
    return (pooled[None, None], totals[0], totals[1], totals[2], totals[3])


def solution(mesh):
    in_specs = (
        P("rep", "samp", None, None, None),
        P("rep", None),
        P("rep", None),
        P("rep", None),
        P(),
        P(),
        P(),
        P(),
        P("rep", "samp", None, None),
    )
    out_specs = (P("rep", "samp", None, None), P(), P(), P(), P())
    return jax.shard_map(
        on_device, mesh=mesh, in_specs=in_specs, out_specs=out_specs, check_vma=False
    )
```

profile of v0, /device:TPU:1, one launch (start us, length us, event | category | flops | bytes accessed | tf_op | source)
XLA Modules:
  0.0 384.8 jit_solution(493478142339106936)
XLA Ops:
  5.4 8.8 %collective-permute-start = (bf16[2,221,8,128]{3,2,1,0:T(8,128)(2,1)}, bf16[2,221,8,128]{3,2,1,0:T(8,128)(2,1)S(1)}, u32[]{:S(2)}, u32[]{:S(2)}) collective-permute-start(bf16[2,221,8,128]{3,2,1,0:T(8,128)(2,1)} %select_select_fusion.1), channel_id=1, source_target_pairs={{0,4},{4,0},{8,12},{12,8},{16,20},{20,16},{24,28},{28,24},{32,36},... | collective-permute-start | bytes 2715656 | tf_op jit(solution)/shard_map/ppermute | solution.py:13
  24.4 2.3 select_select_fusion
  27.4 26.8 %while.39 = (s32[]{:T(128)}, f32[3,64,221]{2,1,0:T(8,128)}, f32[3,221]{1,0:T(4,128)S(1)}, bf16[3,221,64,128]{3,2,1,0:T(8,128)(2,1)}, bf16[3,221,8,128]{3,2,1,0:T...) while((s32[]{:T(128)}, f32[3,64,221]{2,1,0:T(8,128)}, ...), condition=%wide.region_4.5_spmd, body=%wide.region_0.4_spmd.sunk | while | flops 340007392 | bytes 30181084 | solution.py:109
  27.6 3.0 bitcast_dynamic-update-slice_fusion.6
  30.6 2.9 multiply_reduce_fusion.9
  33.6 1.9 multiply_reduce_fusion.10
  36.5 3.0 bitcast_dynamic-update-slice_fusion.6
  39.5 2.9 multiply_reduce_fusion.9
  42.5 1.9 multiply_reduce_fusion.10
  45.4 3.1 bitcast_dynamic-update-slice_fusion.6
  48.4 2.9 multiply_reduce_fusion.9
  51.5 1.9 multiply_reduce_fusion.10
  54.8 18.0 %while.47 = (s32[]{:T(128)}, f32[3,1024]{1,0:T(4,128)S(1)}, s32[3,2]{0,1:T(2,128)S(1)}, f32[3,221]{1,0:T(4,128)S(1)}, s32[]{:T(128)}, /*index=5*/s32[2]{0:T(128)S(1)}) while((s32[]{:T(128)}, f32[3,1024]{1,0:T(4,128)S(1)}, s32[3,2]{0,1:T(2,128)S(1)}, f32[3,221]{1,0:T(4,128)S(1)}, s32[]{:T(128)}, /*index=5*/s32[2]{0:T(128)S(1)}) %tuple.234), condition=%wide.while_cond.7, body=%wide.while_body.7.sunk | while | flops 232 | bytes 4559 | solution.py:78
  55.4 1.9 and_reduce_fusion.11
  77.5 27.7 %while.45 = (s32[]{:T(128)}, f32[3,64,1024]{2,1,0:T(8,128)}, s32[3,3]{1,0:T(4,128)S(1)}, f32[3,64,221]{2,1,0:T(8,128)}, s32[]{:T(128)}, /*index=5*/s32[3]{0:T(128)S(1)}, s32[]{:T(128)}) while((s32[]{:T(128)}, f32[3,64,1024]{2,1,0:T(8,128)}, s32[3,3]{1,0:T(4,128)S(1)}, f32[3,64,221]{2,1,0:T(8,128)}, s32[]{:T(128)}, /*index=5*/s32[3]{0:T(128)S(1)}, ...), condition=%wide.while_cond.5, body=%wide.while_body.5.sunk | while | flops 14163 | bytes 283051 | solution.py:75
  78.1 2.7 and_reduce_fusion.9
  80.8 2.9 dynamic-slice_select_fusion.5
  83.8 2.9 dynamic-update-slice.29
  87.3 2.7 and_reduce_fusion.9
  90.0 2.9 dynamic-slice_select_fusion.5
  93.0 2.9 dynamic-update-slice.29
  96.6 2.7 and_reduce_fusion.9
  99.2 2.9 dynamic-slice_select_fusion.5
  102.2 3.0 dynamic-update-slice.29
  107.1 2.4 collective-permute-start.1
  110.4 27.5 %while.44 = (s32[]{:T(128)}, f32[3,64,1024]{2,1,0:T(8,128)}, s32[3,3]{1,0:T(4,128)S(1)}, f32[3,64,221]{2,1,0:T(8,128)S(1)}, s32[]{:T(128)}, /*index=5*/s32[3]{0:T(128)S(1)}, s32[]{:T(128)}) while((s32[]{:T(128)}, f32[3,64,1024]{2,1,0:T(8,128)}, s32[3,3]{1,0:T(4,128)S(1)}, f32[3,64,221]{2,1,0:T(8,128)S(1)}, s32[]{:T(128)}, ...), condition=%wide.while_cond.4, body=%wide.while_body.4.sunk | while | flops 14163 | bytes 283051 | solution.py:75
  111.1 2.7 and_reduce_fusion.8
  113.7 2.9 dynamic-slice_select_fusion.4
  116.6 3.0 dynamic-update-slice.28
  120.2 2.7 and_reduce_fusion.8
  122.9 2.9 dynamic-slice_select_fusion.4
  125.8 3.0 dynamic-update-slice.28
  129.4 2.7 and_reduce_fusion.8
  132.1 2.9 dynamic-slice_select_fusion.4
  135.0 3.0 dynamic-update-slice.28
  137.9 18.9 %while.46 = (s32[]{:T(128)}, f32[3,1024]{1,0:T(4,128)S(1)}, s32[3,2]{0,1:T(2,128)S(1)}, f32[3,221]{1,0:T(4,128)S(1)}, s32[]{:T(128)}, /*index=5*/s32[2]{0:T(128)S(1)}) while((s32[]{:T(128)}, f32[3,1024]{1,0:T(4,128)S(1)}, s32[3,2]{0,1:T(2,128)S(1)}, f32[3,221]{1,0:T(4,128)S(1)}, s32[]{:T(128)}, /*index=5*/s32[2]{0:T(128)S(1)}) %tuple.235), condition=%wide.while_cond.6, body=%wide.while_body.6.sunk | while | flops 232 | bytes 4559 | solution.py:78
  138.5 2.0 and_reduce_fusion.10
  140.5 2.0 broadcast_select_fusion.8
  144.8 2.0 and_reduce_fusion.10
  146.8 2.0 broadcast_select_fusion.8
  151.1 2.0 and_reduce_fusion.10
  153.1 2.0 broadcast_select_fusion.8
  162.6 2.6 collective-permute-start.3
  165.2 6.7 %while.40 = (s32[]{:T(128)}, f32[64,1024]{1,0:T(8,128)}, s32[3,2]{0,1:T(2,128)S(1)}, f32[3,64,221]{2,1,0:T(8,128)S(1)}, s32[]{:T(128)}) while((s32[]{:T(128)}, f32[64,1024]{1,0:T(8,128)}, s32[3,2]{0,1:T(2,128)S(1)}, f32[3,64,221]{2,1,0:T(8,128)S(1)}, s32[]{:T(128)}) %tuple.214), condition=%wide.while_cond, body=%wide.while_body.sunk | while | flops 2 | bytes 122209 | solution.py:85
  172.8 6.1 %while.42 = (s32[]{:T(128)}, f32[1024]{0:T(1024)}, s32[3,1]{0,1:T(1,128)S(1)}, f32[3,221]{1,0:T(4,128)S(1)}, s32[]{:T(128)}, /*index=5*/s32[]{:T(128)}) while((s32[]{:T(128)}, f32[1024]{0:T(1024)}, s32[3,1]{0,1:T(1,128)S(1)}, f32[3,221]{1,0:T(4,128)S(1)}, s32[]{:T(128)}, /*index=5*/s32[]{:T(128)}) %tuple.220), condition=%wide.while_cond.2, body=%wide.while_body.2.sunk | while | flops 2 | bytes 3625 | solution.py:86
  178.9 4.0 %while.43 = (s32[]{:T(128)}, f32[1024]{0:T(1024)S(1)}, s32[3,1]{0,1:T(1,128)S(1)}, f32[3,221]{1,0:T(4,128)S(1)}, s32[]{:T(128)}, /*index=5*/s32[]{:T(128)}) while((s32[]{:T(128)}, f32[1024]{0:T(1024)S(1)}, s32[3,1]{0,1:T(1,128)S(1)}, f32[3,221]{1,0:T(4,128)S(1)}, s32[]{:T(128)}, /*index=5*/s32[]{:T(128)}) %tuple.239), condition=%wide.while_cond.3, body=%wide.while_body.3.sunk | while | flops 2 | bytes 3625 | solution.py:86
  183.0 6.7 %while.41 = (s32[]{:T(128)}, f32[64,1024]{1,0:T(8,128)}, s32[3,2]{0,1:T(2,128)S(1)}, f32[3,64,221]{2,1,0:T(8,128)S(1)}, s32[]{:T(128)}) while((s32[]{:T(128)}, f32[64,1024]{1,0:T(8,128)}, s32[3,2]{0,1:T(2,128)S(1)}, f32[3,64,221]{2,1,0:T(8,128)S(1)}, s32[]{:T(128)}) %tuple.230), condition=%wide.while_cond.1, body=%wide.while_body.1.sunk | while | flops 2 | bytes 122209 | solution.py:85
  191.8 87.5 %while.48 = (s32[]{:T(128)}, f32[3,8,64]{2,1,0:T(8,128)}, f32[64]{0:T(128)}, f32[64,64]{1,0:T(8,128)S(1)}, f32[64]{0:T(128)}, /*index=5*/bf16[3,221,8,128]{3,2,1...) while((s32[]{:T(128)}, f32[3,8,64]{2,1,0:T(8,128)}, ...), condition=%wide.region_19.20_spmd.clone, body=%wide.region_14.19_spmd.clone.sunk | while | flops 834365952 | bytes 77733992 | solution.py:140
  191.8 6.3 %multiply_reduce_fusion.11 = (f32[221,128]{1,0:T(8,128)S(1)}, f32[221,128]{1,0:T(8,128)S(1)}, f32[221,128,64]{1,2,0:T(8,128)S(1)}) fusion(f32[64]{0:T(128)} %get-tuple-element.1078, f32[221,64]{1,0:T(8,128)S(1)} %dynamic-slice_bitcast_fusion.9, bf16[64,64]{1,0:T(8,128)(2,1)} %get-tuple-element.1077, ...), kind=kOutput, calls=%fused_computation.68.clone.1 | convolution fusion | flops 246162176 | bytes 11162880 | tf_op jit(solution)/shard_map/while/body/eval_jaxpr/pgr,gf->pfr/dot_general | solution.py:36
  198.9 5.8 %multiply_reduce_fusion.12 = (f32[64]{0:T(128)S(1)}, bf16[221,64,128]{2,1,0:T(8,128)(2,1)S(1)}) fusion(f32[221,128]{1,0:T(8,128)S(1)} %get-tuple-element.848, f32[221,128,64]{1,2,0:T(8,128)S(1)} %get-tuple-element.849, f32[64]{0:T(128)S(1)} %copy-done.9, f32[221,128]{1,0:T(8,128)S(1)} %get-tuple-element.850, f32[221,64]{1,0:T(8,128)S(1)} %dynamic-slice_bitcast_fusion.9), kind=kLoop, calls=%fused_computation.65.clone.1 | loop fusion | flops 27156416 | bytes 11145984 | tf_op jit(solution)/shard_map/while/body/eval_jaxpr/reduce_sum | solution.py:58
  206.6 5.9 %convert_reduce_fusion.2 = (f32[64]{0:T(128)}, bf16[221,64,128]{2,1,0:T(8,128)(2,1)}) fusion(bf16[221,64,128]{2,1,0:T(8,128)(2,1)S(1)} %get-tuple-element.851, bf16[64,64]{1,0:T(8,128)(2,1)S(1)} %copy-done.7, bf16[3,221,64,128]{3,2,1,0:T(8,128)(2,1)} %get-tuple-element.1075, s32[]{:T(128)} %get-tuple-element.1055), kind=kOutput, calls=%fused_computation.66.clone.1 | convolution fusion | flops 240787392 | bytes 10871044 | tf_op jit(solution)/shard_map/while/body/eval_jaxpr/pfr,gf->pgr/dot_general | solution.py:64
  214.1 3.7 fusion.119
  217.8 3.1 fusion.121
  221.0 6.3 %multiply_reduce_fusion.11 = (f32[221,128]{1,0:T(8,128)S(1)}, f32[221,128]{1,0:T(8,128)S(1)}, f32[221,128,64]{1,2,0:T(8,128)S(1)}) fusion(f32[64]{0:T(128)} %get-tuple-element.1078, f32[221,64]{1,0:T(8,128)S(1)} %dynamic-slice_bitcast_fusion.9, bf16[64,64]{1,0:T(8,128)(2,1)} %get-tuple-element.1077, ...), kind=kOutput, calls=%fused_computation.68.clone.1 | convolution fusion | flops 246162176 | bytes 11162880 | tf_op jit(solution)/shard_map/while/body/eval_jaxpr/pgr,gf->pfr/dot_general | solution.py:36
  228.1 5.8 %multiply_reduce_fusion.12 = (f32[64]{0:T(128)S(1)}, bf16[221,64,128]{2,1,0:T(8,128)(2,1)S(1)}) fusion(f32[221,128]{1,0:T(8,128)S(1)} %get-tuple-element.848, f32[221,128,64]{1,2,0:T(8,128)S(1)} %get-tuple-element.849, f32[64]{0:T(128)S(1)} %copy-done.9, f32[221,128]{1,0:T(8,128)S(1)} %get-tuple-element.850, f32[221,64]{1,0:T(8,128)S(1)} %dynamic-slice_bitcast_fusion.9), kind=kLoop, calls=%fused_computation.65.clone.1 | loop fusion | flops 27156416 | bytes 11145984 | tf_op jit(solution)/shard_map/while/body/eval_jaxpr/reduce_sum | solution.py:58
  235.8 5.9 %convert_reduce_fusion.2 = (f32[64]{0:T(128)}, bf16[221,64,128]{2,1,0:T(8,128)(2,1)}) fusion(bf16[221,64,128]{2,1,0:T(8,128)(2,1)S(1)} %get-tuple-element.851, bf16[64,64]{1,0:T(8,128)(2,1)S(1)} %copy-done.7, bf16[3,221,64,128]{3,2,1,0:T(8,128)(2,1)} %get-tuple-element.1075, s32[]{:T(128)} %get-tuple-element.1055), kind=kOutput, calls=%fused_computation.66.clone.1 | convolution fusion | flops 240787392 | bytes 10871044 | tf_op jit(solution)/shard_map/while/body/eval_jaxpr/pfr,gf->pgr/dot_general | solution.py:64
  243.2 3.7 fusion.119
  247.0 3.1 fusion.121
  250.1 6.3 %multiply_reduce_fusion.11 = (f32[221,128]{1,0:T(8,128)S(1)}, f32[221,128]{1,0:T(8,128)S(1)}, f32[221,128,64]{1,2,0:T(8,128)S(1)}) fusion(f32[64]{0:T(128)} %get-tuple-element.1078, f32[221,64]{1,0:T(8,128)S(1)} %dynamic-slice_bitcast_fusion.9, bf16[64,64]{1,0:T(8,128)(2,1)} %get-tuple-element.1077, ...), kind=kOutput, calls=%fused_computation.68.clone.1 | convolution fusion | flops 246162176 | bytes 11162880 | tf_op jit(solution)/shard_map/while/body/eval_jaxpr/pgr,gf->pfr/dot_general | solution.py:36
  257.3 5.8 %multiply_reduce_fusion.12 = (f32[64]{0:T(128)S(1)}, bf16[221,64,128]{2,1,0:T(8,128)(2,1)S(1)}) fusion(f32[221,128]{1,0:T(8,128)S(1)} %get-tuple-element.848, f32[221,128,64]{1,2,0:T(8,128)S(1)} %get-tuple-element.849, f32[64]{0:T(128)S(1)} %copy-done.9, f32[221,128]{1,0:T(8,128)S(1)} %get-tuple-element.850, f32[221,64]{1,0:T(8,128)S(1)} %dynamic-slice_bitcast_fusion.9), kind=kLoop, calls=%fused_computation.65.clone.1 | loop fusion | flops 27156416 | bytes 11145984 | tf_op jit(solution)/shard_map/while/body/eval_jaxpr/reduce_sum | solution.py:58
  265.0 5.9 %convert_reduce_fusion.2 = (f32[64]{0:T(128)}, bf16[221,64,128]{2,1,0:T(8,128)(2,1)}) fusion(bf16[221,64,128]{2,1,0:T(8,128)(2,1)S(1)} %get-tuple-element.851, bf16[64,64]{1,0:T(8,128)(2,1)S(1)} %copy-done.7, bf16[3,221,64,128]{3,2,1,0:T(8,128)(2,1)} %get-tuple-element.1075, s32[]{:T(128)} %get-tuple-element.1055), kind=kOutput, calls=%fused_computation.66.clone.1 | convolution fusion | flops 240787392 | bytes 10871044 | tf_op jit(solution)/shard_map/while/body/eval_jaxpr/pfr,gf->pgr/dot_general | solution.py:64
  272.4 3.7 fusion.119
  276.1 3.1 fusion.121
  279.3 105.5 %all-reduce.5 = (f32[3,8,64]{2,1,0:T(8,128)}, f32[64]{0:T(128)}, f32[64,64]{1,0:T(8,128)}, f32[64]{0:T(128)}) all-reduce(f32[3,8,64]{2,1,0:T(8,128)} %get-tuple-element.127, f32[64]{0:T(128)} %get-tuple-element.128, f32[64,64]{1,0:T(8,128)S(1)} %get-tuple-element.129, ...), channel_id=1, replica_groups=mesh['samp'=128,'rep'=4] {'samp','rep'}, use_global_device_ids=true, to_apply=%region_20.21 | all-reduce | flops 5760 | bytes 46080 | tf_op jit(solution)/shard_map/psum | solution.py:231
  (221 shorter events, 96.1 us)
Async XLA Ops:
  0.6 2.2 copy-start
  0.6 19.5 %copy-start.3 = (s32[1,512]{1,0:T(1,128)S(1)}, s32[1,512]{1,0:T(1,128)}, u32[]{:S(2)}) copy-start(s32[1,512]{1,0:T(1,128)} %param.15) | copy-start | bytes 6148
  0.7 20.1 %copy-start.6 = (bf16[64,64]{1,0:T(8,128)(2,1)S(1)}, bf16[64,64]{1,0:T(8,128)(2,1)}, u32[]{:S(2)}) copy-start(bf16[64,64]{1,0:T(8,128)(2,1)} %param.19) | copy-start | bytes 24580
  2.8 24.6 %copy-start.8 = (f32[64]{0:T(128)S(1)}, f32[64]{0:T(128)}, u32[]{:S(2)}) copy-start(f32[64]{0:T(128)} %param.20) | copy-start | bytes 772
  2.8 24.6 %copy-start.12 = (bf16[3,8,64]{2,1,0:T(8,128)(2,1)S(1)}, bf16[3,8,64]{2,1,0:T(8,128)(2,1)}, u32[]{:S(2)}) copy-start(bf16[3,8,64]{2,1,0:T(8,128)(2,1)} %param.17) | copy-start | bytes 9220
  2.8 24.6 %copy-start.13 = (f32[64]{0:T(128)S(1)}, f32[64]{0:T(128)}, u32[]{:S(2)}) copy-start(f32[64]{0:T(128)} %param.18) | copy-start | bytes 772
  5.4 17.1 %collective-permute-start = (bf16[2,221,8,128]{3,2,1,0:T(8,128)(2,1)}, bf16[2,221,8,128]{3,2,1,0:T(8,128)(2,1)S(1)}, u32[]{:S(2)}, u32[]{:S(2)}) collective-permute-start(bf16[2,221,8,128]{3,2,1,0:T(8,128)(2,1)} %select_select_fusion.1), channel_id=1, source_target_pairs={{0,4},{4,0},{8,12},{12,8},{16,20},{20,16},{24,28},{28,24},{32,36},... | collective-permute-start | bytes 2715656 | tf_op jit(solution)/shard_map/ppermute | solution.py:13
  16.9 166.0 %copy-start.10 = (pred[3]{0:T(512)(128)(4,1)}, pred[3]{0:T(512)(128)(4,1)S(1)}, u32[]{:S(2)}) copy-start(pred[3]{0:T(512)(128)(4,1)S(1)} %get-tuple-element.405) | copy-start | bytes 13
  27.4 27.4 %copy-start.5 = (s32[2]{0:T(128)S(1)}, s32[2]{0:T(128)}, u32[]{:S(2)}) copy-start(s32[2]{0:T(128)} %constant.489) | copy-start | bytes 28
  27.4 50.1 %copy-start.4 = (s32[3]{0:T(128)S(1)}, s32[3]{0:T(128)}, u32[]{:S(2)}) copy-start(s32[3]{0:T(128)} %constant.465) | copy-start | bytes 40
  54.2 0.6 copy-start.11
  72.9 85.2 %collective-permute-start.2 = (f32[1024]{0:T(1024)S(1)}, f32[1024]{0:T(1024)S(1)}, u32[]{:S(2)}, u32[]{:S(2)}) collective-permute-start(f32[1024]{0:T(1024)S(1)} %reduce_sum.111), channel_id=1, source_target_pairs={{0,4},{4,0},{8,12},{12,8},{16,20},{20,16},{24,28},{28,24},{32,36},... | collective-permute-start | bytes 12296 | tf_op jit(solution)/shard_map/ppermute | solution.py:13
  107.1 51.1 %collective-permute-start.1 = (f32[64,1024]{1,0:T(8,128)}, f32[64,1024]{1,0:T(8,128)}, u32[]{:S(2)}, u32[]{:S(2)}) collective-permute-start(f32[64,1024]{1,0:T(8,128)} %reduce_sum.109), channel_id=1, source_target_pairs={{0,4},{4,0},{8,12},{12,8},{16,20},{20,16},{24,28},{28,24},{32,36},... | collective-permute-start | bytes 786440 | tf_op jit(solution)/shard_map/ppermute | solution.py:13
  160.6 18.2 %collective-permute-start.4 = (f32[1024]{0:T(1024)}, f32[1024]{0:T(1024)S(1)}, u32[]{:S(2)}, u32[]{:S(2)}) collective-permute-start(f32[1024]{0:T(1024)} %divide_select_fusion), channel_id=1, source_target_pairs={{0,4},{4,0},{8,12},{12,8},{16,20},{20,16},{24,28},{28,24},{32,36},... | collective-permute-start | bytes 12296 | tf_op jit(solution)/shard_map/ppermute | solution.py:13
  162.6 20.4 %collective-permute-start.3 = (f32[64,1024]{1,0:T(8,128)}, f32[64,1024]{1,0:T(8,128)}, u32[]{:S(2)}, u32[]{:S(2)}) collective-permute-start(f32[64,1024]{1,0:T(8,128)} %get-tuple-element.976), channel_id=1, source_target_pairs={{0,4},{4,0},{8,12},{12,8},{16,20},{20,16},{24,28},{28,24},{32,36},... | collective-permute-start | bytes 786440 | tf_op jit(solution)/shard_map/ppermute | solution.py:13
  191.8 7.1 %copy-start.9 = (f32[64]{0:T(128)S(1)}, f32[64]{0:T(128)}, u32[]{:S(2)}) copy-start(f32[64]{0:T(128)} %get-tuple-element.1078) | copy-start | bytes 772 | tf_op jit(solution)/shard_map/while
  198.1 8.6 %copy-start.7 = (bf16[64,64]{1,0:T(8,128)(2,1)S(1)}, bf16[64,64]{1,0:T(8,128)(2,1)}, u32[]{:S(2)}) copy-start(bf16[64,64]{1,0:T(8,128)(2,1)} %get-tuple-element.1077) | copy-start | bytes 24580 | tf_op jit(solution)/shard_map/while
  204.8 1.9 copy-start.1
  212.6 5.2 %copy-start.2 = (bf16[221,64,128]{2,1,0:T(8,128)(2,1)S(1)}, bf16[221,64,128]{2,1,0:T(8,128)(2,1)}, u32[]{:S(2)}) copy-start(bf16[221,64,128]{2,1,0:T(8,128)(2,1)} %copy-done.1) | copy-start | bytes 10862596 | tf_op jit(solution)/shard_map/while
  220.9 7.1 %copy-start.9 = (f32[64]{0:T(128)S(1)}, f32[64]{0:T(128)}, u32[]{:S(2)}) copy-start(f32[64]{0:T(128)} %get-tuple-element.1078) | copy-start | bytes 772 | tf_op jit(solution)/shard_map/while
  227.2 8.6 %copy-start.7 = (bf16[64,64]{1,0:T(8,128)(2,1)S(1)}, bf16[64,64]{1,0:T(8,128)(2,1)}, u32[]{:S(2)}) copy-start(bf16[64,64]{1,0:T(8,128)(2,1)} %get-tuple-element.1077) | copy-start | bytes 24580 | tf_op jit(solution)/shard_map/while
  233.9 1.9 copy-start.1
  241.7 5.3 %copy-start.2 = (bf16[221,64,128]{2,1,0:T(8,128)(2,1)S(1)}, bf16[221,64,128]{2,1,0:T(8,128)(2,1)}, u32[]{:S(2)}) copy-start(bf16[221,64,128]{2,1,0:T(8,128)(2,1)} %copy-done.1) | copy-start | bytes 10862596 | tf_op jit(solution)/shard_map/while
  250.1 7.1 %copy-start.9 = (f32[64]{0:T(128)S(1)}, f32[64]{0:T(128)}, u32[]{:S(2)}) copy-start(f32[64]{0:T(128)} %get-tuple-element.1078) | copy-start | bytes 772 | tf_op jit(solution)/shard_map/while
  256.4 8.6 %copy-start.7 = (bf16[64,64]{1,0:T(8,128)(2,1)S(1)}, bf16[64,64]{1,0:T(8,128)(2,1)}, u32[]{:S(2)}) copy-start(bf16[64,64]{1,0:T(8,128)(2,1)} %get-tuple-element.1077) | copy-start | bytes 24580 | tf_op jit(solution)/shard_map/while
  263.1 1.9 copy-start.1
  270.9 5.3 %copy-start.2 = (bf16[221,64,128]{2,1,0:T(8,128)(2,1)S(1)}, bf16[221,64,128]{2,1,0:T(8,128)(2,1)}, u32[]{:S(2)}) copy-start(bf16[221,64,128]{2,1,0:T(8,128)(2,1)} %copy-done.1) | copy-start | bytes 10862596 | tf_op jit(solution)/shard_map/while
where the time goes:
time: 388 us; the launch traced here: 385 us
  blocking collectives  106 us (27%)
  other arithmetic  101 us (26%)
  local copies, waits for them, and re-layouts  82.3 us (21%)
  matrix products  74.8 us (19%)
  starting transfers between devices  17.6 us (5%)
    psum x1, blocking collectives, on_device(): lax.psum((gradients[0], gradients[1], gradients[2], gradients[3]), ('samp...  106 us
    scatter x24, other arithmetic  57 us
    scatter x36, local copies, waits for them, and re-layouts  34.9 us
    dot_general x6, matrix products, second_layer(): jnp.einsum('pgr,gf->pfr', hidden, mix_weight, preferred_element_type=jnp....  27.5 us
    gather x36, local copies, waits for them, and re-layouts  23.4 us
    dot_general x3, matrix products, backward_slot(): jnp.einsum('pfr,gf->pgr', d_second, mix_weight, preferred_element_type=jn...  17.7 us
    ppermute x5, starting transfers between devices, partner_2(): return lax.ppermute(value, axis, pairs)  17.6 us
    reduce_sum x3, other arithmetic, backward_slot(): g_query = jnp.sum(d_score[:, None, :] * feature, axis=(0, 2))  17.5 us
  transfers between devices with their start and end apart: 5, of which 0 were waited for; matrix products, arithmetic and copies ran while one was open for 27% of the time, Pallas kernels for 0%

commit v1 on v0

v1 whole, which is shorter than its diff:
```python
import jax
import jax.numpy as jnp
from jax import lax
from jax.experimental import pallas as pl
from jax.experimental.pallas import tpu as pltpu
from jax.sharding import PartitionSpec as P

POS = 221
CH = 8
R = 128
F = 64
OWN = 4
SITES = 1024
HALF = 112
GROUP = 8
CHUNKS = HALF // GROUP
XPOS = 2 * HALF + 2
WIN = SITES + 8
SPARE = OWN * CHUNKS

F32 = jnp.float32
BF = jnp.bfloat16
NT = (((1,), (1,)), ((), ()))


def mm(a, b):
    return jnp.dot(a, b, preferred_element_type=F32)


def mm_nt(a, b):
    return lax.dot_general(a, b, NT, preferred_element_type=F32)


def split2(v):
    hi = v.astype(BF)
    return hi, (v - hi.astype(F32)).astype(BF)


def halves(v):
    zero = jnp.zeros((8, R), v.dtype)
    left = jnp.concatenate([v[:, :R], zero], axis=1)
    right = jnp.concatenate([zero, v[:, R:]], axis=1)
    return jnp.concatenate([left, right], axis=0)


def pooling_kernel(
    dev, counts, reads, starts, x, conv_w, bias, mix, query, cot,
    pooled, grads,
    hid, feat, slope, weight_rows, gate_rows, score_rows, second_ring, relu_ring,
    w_num, w_den, d_num, d_den, acc_mix, acc_conv, acc_query,
):
    me = dev[0]
    count = counts[0, me]
    total = count * CHUNKS

    zeros = lambda *s: jnp.zeros(s, F32)
    cw = conv_w[...].astype(F32)
    b = bias[...]
    b_hi = b.astype(BF).astype(F32)
    b_mid = (b - b_hi).astype(BF).astype(F32)
    b_lo = b - b_hi - b_mid
    b_rows = jnp.concatenate([b_hi, b_mid, b_lo, zeros(13, F)], axis=0)
    even = jnp.concatenate([cw, zeros(8, F), b_rows, zeros(80, F)], axis=0)
    odd = jnp.concatenate([zeros(8, F), cw, b_rows, zeros(80, F)], axis=0)
    conv_lhs = jnp.concatenate([even.T, odd.T], axis=0)[:, :48].astype(BF)
    mix_f = mix[...].astype(F32)
    pad_mix = jnp.concatenate([mix_f, zeros(64, F)], axis=0)
    mix_t = (0.5 * pad_mix.T[:, :F]).astype(BF)
    mix_b = mix[...]
    q = 0.5 * query[...]
    q_hi = q.astype(BF).astype(F32)
    q_lo = q - q_hi
    q_hi8 = jnp.broadcast_to(q_hi, (8, F))
    q_lo8 = jnp.broadcast_to(q_lo, (8, F))
    query_lhs = jnp.concatenate([q_hi8, q_lo8], axis=0).astype(BF)
    ones = jnp.ones((16, 2 * R), BF)
    row8 = lax.broadcasted_iota(jnp.int32, (8, 2 * R), 0)
    lane8 = lax.broadcasted_iota(jnp.int32, (8, 2 * R), 1)
    row16 = lax.broadcasted_iota(jnp.int32, (16, F), 0)
    lane_mod = lax.broadcasted_iota(jnp.int32, (F, 128), 1) % GROUP

    def place(k):
        slot = jnp.minimum(k // CHUNKS, OWN - 1)
        return slot, k - (k // CHUNKS) * CHUNKS

    def window(slot, c, i):
        base = pl.multiple_of(c * (GROUP * CH), 16)
        left = x[slot, pl.ds(base + 16 * i, 32), :]
        right = x[slot, pl.ds(base + HALF * CH + 16 * i, 32), :]
        return jnp.concatenate(
            [jnp.concatenate([left, right], axis=1), ones], axis=0
        )

    w_num[...] = jnp.zeros(w_num.shape, F32)
    w_den[...] = jnp.zeros(w_den.shape, F32)

    def first_stage(k):
        slot, c = place(k)
        for i in range(GROUP // 2):
            pre = mm(conv_lhs, window(slot, c, i))
            hid[k, 128 * i : 128 * i + 128, :] = jnp.maximum(pre, 0.0).astype(BF)

    def second_stage(k):
        for j in range(GROUP):
            rows = slice(F * j, F * j + F)
            h = mm(mix_t, hid[k, rows, :])
            t = jnp.tanh(h)
            u = h * t
            feat[k, rows, :] = (h + u).astype(BF)
            slope[k, rows, :] = ((1.0 + t) * (1.0 + (h - u))).astype(BF)

    def score_stage(k):
        slot, c = place(k)
        score = jnp.zeros((8, 2 * R), F32)
        for j in range(GROUP):
            s = mm(query_lhs, feat[k, F * j : F * j + F, :])
            score = jnp.where(row8 == j, s[:8] + s[8:], score)
        opening = 0.5 + 0.5 * jnp.tanh(score)
        read = jnp.where(lane8 < R, lane8, lane8 - R)
        position = jnp.where(lane8 < R, row8, row8 + HALF) + GROUP * c
        live = (read < reads[0, me * OWN + slot]) & (position < POS)
        weight = jnp.where(live, opening, 0.0)
        weight_rows[k] = weight
        gate_rows[k] = weight * (1.0 - opening)

    def pool_stage(k, valid):
        slot, c = place(k)
        weight = weight_rows[k]
        lhs = halves(weight).astype(BF)
        num = jnp.zeros((16, F), F32)
        for j in range(GROUP):
            n = mm_nt(lhs, feat[k, F * j : F * j + F, :])
            num = jnp.where((row16 % GROUP) == j, n, num)
        den_l = jnp.sum(weight[:, :R], axis=1, keepdims=True)
        den_r = jnp.sum(weight[:, R:], axis=1, keepdims=True)
        first = starts[0, me * OWN + slot] + GROUP * c
        for part, den, at in ((num[:8], den_l, first), (num[8:], den_r, first + HALF)):
            here = pl.ds(at, 8)
            w_num[here, :] += jnp.where(valid, part, 0.0)
            w_den[here, :] += jnp.where(valid, jnp.broadcast_to(den, (8, 128)), 0.0)

    @pl.loop(0, total + 3)
    def _(i):
        pool_stage(jnp.maximum(i - 3, 0), i >= 3)
        score_stage(jnp.clip(i - 2, 0, SPARE))
        second_stage(jnp.clip(i - 1, 0, SPARE))
        first_stage(jnp.minimum(i, SPARE))

    d_num[SITES:, :] = jnp.zeros((WIN - SITES, 128), F32)
    d_den[SITES:, :] = jnp.zeros((WIN - SITES, 128), F32)

    @pl.loop(0, SITES // 128)
    def _(i):
        at = pl.multiple_of(i * 128, 128)
        here = pl.ds(at, 128)
        num = w_num[here, :]
        den = w_den[here, :]
        safe = jnp.maximum(den, 1.0)
        inv = 1.0 / safe
        inv_f = inv[:, :F]
        out = jnp.concatenate([num * inv_f, jnp.zeros((128, F), F32)], axis=1)
        pooled[:, here] = out.T[:F]
        cot_t = jnp.concatenate([cot[:, here], jnp.zeros((F, 128), F32)], axis=0).T
        dn = cot_t * inv
        d_num[here, :] = dn
        inner = jnp.sum(dn[:, :F] * num, axis=1, keepdims=True)
        d_den[here, :] = jnp.where(den > 1.0, -(jnp.broadcast_to(inner, (128, 128)) * inv), 0.0)

    acc_mix[...] = jnp.zeros(acc_mix.shape, F32)
    acc_conv[...] = jnp.zeros(acc_conv.shape, F32)
    acc_query[...] = jnp.zeros(acc_query.shape, F32)

    def cut(k):
        slot, c = place(k)
        first = starts[0, me * OWN + slot] + GROUP * c
        return first, jnp.concatenate(
            [d_num[pl.ds(first, 8), :], d_num[pl.ds(first + HALF, 8), :]], axis=0
        )

    def weight_stage(k):
        first, dn = cut(k)
        hi, lo = split2(dn[:, :F])
        lhs = jnp.concatenate([hi, lo], axis=0)
        d_weight = jnp.zeros((8, 2 * R), F32)
        for j in range(GROUP):
            w = mm(lhs, feat[k, F * j : F * j + F, :])
            w = w[:16] + w[16:]
            w = jnp.concatenate([w[:8, :R], w[8:, R:]], axis=1)
            d_weight = jnp.where(row8 == j, w, d_weight)
        dd = jnp.concatenate([d_den[pl.ds(first, 8), :], d_den[pl.ds(first + HALF, 8), :]], axis=1)
        score_rows[k % 4] = (d_weight + dd) * gate_rows[k]

    def second_back(k):
        _, dn = cut(k)
        half = 0.5 * dn
        hi = half.astype(BF).astype(F32)
        lo = half - hi
        pad_q = lambda v: jnp.concatenate([jnp.broadcast_to(v, (16, F)), zeros(16, F)], axis=1)
        lhs_t = jnp.concatenate(
            [hi, hi, lo, pad_q(q_hi), pad_q(q_hi), pad_q(q_lo), zeros(32, 128)], axis=0
        )
        lhs = lhs_t.T[:F]
        w_hi, w_lo = split2(weight_rows[k])
        s_hi, s_lo = split2(score_rows[k % 4])
        w_hi, w_lo, s_hi, s_lo = halves_bf(w_hi), halves_bf(w_lo), halves_bf(s_hi), halves_bf(s_lo)
        rhs = jnp.concatenate([w_hi, w_lo, w_hi, s_hi, s_lo, s_hi], axis=0)
        for j in range(GROUP):
            rows = slice(F * j, F * j + F)
            part = jnp.where(lane_mod == j, lhs, 0.0).astype(BF)[:, :96]
            d_feat = mm(part, rhs)
            second_ring[k % 2, rows, :] = (d_feat * slope[k, rows, :].astype(F32)).astype(BF)

    def halves_bf(v):
        return halves(v.astype(F32)).astype(BF)

    def relu_back(k, valid):
        lhs, rhs = [], []
        for j in range(GROUP):
            rows = slice(F * j, F * j + F)
            d2 = second_ring[k % 2, rows, :]
            h = hid[k, rows, :]
            lhs.append(h)
            rhs.append(d2)
            dh = mm(mix_b, d2).astype(BF)
            relu_ring[k % 2, rows, :] = jnp.where(h > 0, dh, jnp.zeros_like(dh))
        g = mm_nt(jnp.concatenate(lhs, axis=1), jnp.concatenate(rhs, axis=1))
        acc_mix[...] += jnp.where(valid, g, 0.0)

    def weights_back(k, valid):
        slot, c = place(k)
        wins = [window(slot, c, i) for i in range(GROUP // 2)]
        lhs = jnp.concatenate(
            [relu_ring[k % 2, 128 * i : 128 * i + 128, :] for i in range(GROUP // 2)], axis=1
        )
        g = mm_nt(lhs, jnp.concatenate(wins, axis=1))
        acc_conv[...] += jnp.where(valid, g, 0.0)
        ds = halves(score_rows[k % 4])
        row = lax.broadcasted_iota(jnp.int32, (16, 2 * R), 0) % GROUP
        lhs, rhs = [], []
        for j in range(GROUP):
            hi, lo = split2(jnp.where(row == j, ds, 0.0))
            lhs.append(jnp.concatenate([hi, lo], axis=0))
            rhs.append(feat[k, F * j : F * j + F, :])
        g = mm_nt(jnp.concatenate(lhs, axis=1), jnp.concatenate(rhs, axis=1))
        acc_query[...] += jnp.where(valid, g, 0.0)

    @pl.loop(0, total + 3)
    def _(i):
        weights_back(jnp.maximum(i - 3, 0), i >= 3)
        relu_back(jnp.clip(i - 2, 0, SPARE - 1), (i >= 2) & (i < total + 2))
        second_back(jnp.clip(i - 1, 0, SPARE - 1))
        weight_stage(jnp.minimum(i, SPARE - 1))

    turned = jnp.concatenate([acc_conv[...], zeros(128, 80)], axis=1).T
    g_conv = turned[0:24, :F] + turned[8:32, F:]
    g_bias = turned[32:33, :F] + turned[32:33, F:]
    g_query = jnp.sum(acc_query[...], axis=0, keepdims=True)
    rest = jnp.concatenate([g_conv, g_bias, g_query, zeros(6, F)], axis=0)
    gm = acc_mix[...]
    grads[0:32, :] = jnp.concatenate([gm[:32], gm[32:]], axis=1)
    grads[32:48, :] = jnp.concatenate([rest[:16], rest[16:]], axis=1)


def run_kernel(dev, counts, reads, starts, x, conv_w, bias, mix, query, cot, interpret=False):
    smem = pl.BlockSpec(memory_space=pltpu.SMEM)
    vmem = pl.BlockSpec(memory_space=pltpu.VMEM)
    big = (SPARE + 1, GROUP * F, 2 * R)
    return pl.pallas_call(
        pooling_kernel,
        out_shape=(
            jax.ShapeDtypeStruct((F, SITES), F32),
            jax.ShapeDtypeStruct((48, 128), F32),
        ),
        in_specs=[smem] * 4 + [vmem] * 6,
        out_specs=(vmem, vmem),
        scratch_shapes=[
            pltpu.VMEM(big, BF),
            pltpu.VMEM(big, BF),
            pltpu.VMEM(big, BF),
            pltpu.VMEM((SPARE + 1, 8, 2 * R), F32),
            pltpu.VMEM((SPARE + 1, 8, 2 * R), F32),
            pltpu.VMEM((4, 8, 2 * R), F32),
            pltpu.VMEM((2, GROUP * F, 2 * R), BF),
            pltpu.VMEM((2, GROUP * F, 2 * R), BF),
            pltpu.VMEM((WIN, F), F32),
            pltpu.VMEM((WIN, 128), F32),
            pltpu.VMEM((WIN, 128), F32),
            pltpu.VMEM((WIN, 128), F32),
            pltpu.VMEM((F, F), F32),
            pltpu.VMEM((128, 48), F32),
            pltpu.VMEM((32, F), F32),
        ],
        compiler_params=pltpu.CompilerParams(vmem_limit_bytes=60 * 2**20),
        interpret=interpret,
    )(dev, counts, reads, starts, x, conv_w, bias, mix, query, cot)


def pad_blocks(blocks):
    padded = jnp.pad(blocks, ((0, 0), (1, XPOS - POS - 1), (0, 0), (0, 0)))
    return padded.reshape(OWN, XPOS * CH, R)


def on_device(
    read_blocks, block_counts, block_reads, block_starts,
    conv_weight, conv_bias, mix_weight, pool_query, site_cotangent,
):
    dev = lax.axis_index("samp").astype(jnp.int32).reshape(1)
    pooled, grads = run_kernel(
        dev, block_counts, block_reads, block_starts,
        pad_blocks(read_blocks[0]),
        conv_weight.reshape(3 * CH, F), conv_bias.reshape(1, F), mix_weight,
        pool_query.reshape(1, F), site_cotangent[0, 0],
    )
    for bit in range(7):
        stride = 1 << bit
        grads = grads + lax.ppermute(grads, "samp", [(i, i ^ stride) for i in range(128)])
    for bit in range(2):
        stride = 1 << bit
        grads = grads + lax.ppermute(grads, "rep", [(i, i ^ stride) for i in range(4)])
    g_mix = jnp.concatenate([grads[:32, :F], grads[:32, F:]], axis=0)
    rest = jnp.concatenate([grads[32:, :F], grads[32:, F:]], axis=0)
    return (pooled[None, None], rest[:24].reshape(3, CH, F), rest[24], g_mix, rest[25])


def solution(mesh):
    in_specs = (
        P("rep", "samp", None, None, None),
        P("rep", None),
        P("rep", None),
        P("rep", None),
        P(),
        P(),
        P(),
        P(),
        P("rep", "samp", None, None),
    )
    out_specs = (P("rep", "samp", None, None), P(), P(), P(), P())
    return jax.shard_map(
        on_device, mesh=mesh, in_specs=in_specs, out_specs=out_specs, check_vma=False
    )
```

time: 388 us -> 137 us (0.35)
  the two profiles are of different devices: /device:TPU:1 before, /device:TPU:2 now
where the time goes in v1:
time: 137 us; the launch traced here: 136 us
  Pallas kernels  60.8 us (44%)
  starting transfers between devices  38.3 us (28%)
  waiting for transfers between devices  31 us (23%)
  local copies, waits for them, and re-layouts  3.62 us (3%)
  other arithmetic  2 us (1%)
    pallas_call x1, Pallas kernels, run_kernel(): pl.pallas_call(pooling_kernel, out_shape=(jax.ShapeDtypeStruct((F, SITES)...  60.8 us
    ppermute x7, starting transfers between devices, on_device(): lax.ppermute(grads, 'samp', [(i, i ^ stride) for i in range(128)])  32 us
    ppermute x7, waiting for transfers between devices, on_device(): lax.ppermute(grads, 'samp', [(i, i ^ stride) for i in range(128)])  24.4 us
    ppermute x2, waiting for transfers between devices, on_device(): lax.ppermute(grads, 'rep', [(i, i ^ stride) for i in range(4)])  6.64 us
    ppermute x2, starting transfers between devices, on_device(): lax.ppermute(grads, 'rep', [(i, i ^ stride) for i in range(4)])  6.26 us
    reshape x1, local copies, waits for them, and re-layouts, pad_blocks(): return padded.reshape(OWN, XPOS * CH, R)  2.89 us
  transfers between devices with their start and end apart: 9, of which 9 were waited for; matrix products, arithmetic and copies ran while one was open for 0% of the time, Pallas kernels for 0%

profile of v1, /device:TPU:2, one launch (start us, length us, event | category | flops | bytes accessed | tf_op | source)
XLA Modules:
  0.0 136.4 jit_solution(882222105799739203)
XLA Ops:
  0.6 2.9 %pad_bitcast_fusion.x = bf16[4,1808,128]{2,1,0:T(8,128)(2,1)} fusion(bf16[4,221,8,128]{3,2,1,0:T(8,128)(2,1)} %bitcast.15), kind=kLoop, calls=%fused_computation | loop fusion | bytes 3661824 | tf_op jit(solution)/shard_map/reshape | solution.py:300
  3.5 60.8 %shard_map.128 = (f32[64,1024]{1,0:T(8,128)}, f32[48,128]{1,0:T(8,128)}) custom-call(s32[1]{0:T(128)} %bitcast.dev, s32[1,128]{1,0:T(1,128)} %counts.1, s32[1,512]{1,0:T(1,128)} %reads.1, s32[1,512]{1,0:T(1,128)} %starts.1, bf16[4,1808,128]{2,1,0:T(8,128)(2,1)} %pad_bitcast_fusion.x, bf16[24,64]{1,0:T(8,128)(2,1)} %bitcast.17, f32[1,64]{1,0:T(1,128)} %bitcast.18, ...), custom_call_target="tpu_custom_call" | custom-call | tf_op jit(solution)/shard_map/pallas_call | solution.py:268
  64.3 1.9 %collective-permute-start = (f32[48,128]{1,0:T(8,128)}, f32[48,128]{1,0:T(8,128)S(1)}, u32[]{:S(2)}, u32[]{:S(2)}) collective-permute-start(f32[48,128]{1,0:T(8,128)} %get-tuple-element.8), channel_id=1, source_target_pairs={{0,4},{4,0},{8,12},{12,8},{16,20},{20,16},{24,28},{28,24},{32,36},... | collective-permute-start | bytes 73736 | tf_op jit(solution)/shard_map/ppermute | solution.py:316
  66.2 1.4 %collective-permute-done = f32[48,128]{1,0:T(8,128)S(1)} collective-permute-done((f32[48,128]{1,0:T(8,128)}, f32[48,128]{1,0:T(8,128)S(1)}, u32[]{:S(2)}, u32[]{:S(2)}) %collective-permute-start) | collective-permute-done | bytes 24608 | tf_op jit(solution)/shard_map/ppermute | solution.py:316
  67.6 0.7 add.29
  68.4 7.8 %collective-permute-start.1 = (f32[48,128]{1,0:T(8,128)S(1)}, f32[48,128]{1,0:T(8,128)S(1)}, u32[]{:S(2)}, u32[]{:S(2)}) collective-permute-start(f32[48,128]{1,0:T(8,128)S(1)} %add.29), channel_id=1, source_target_pairs={{0,8},{4,12},{8,0},{12,4},{16,24},{20,28},{24,16},{28,20},{32,40},... | collective-permute-start | bytes 73736 | tf_op jit(solution)/shard_map/ppermute | solution.py:316
  76.1 1.8 %collective-permute-done.1 = f32[48,128]{1,0:T(8,128)S(1)} collective-permute-done((f32[48,128]{1,0:T(8,128)S(1)}, f32[48,128]{1,0:T(8,128)S(1)}, u32[]{:S(2)}, u32[]{:S(2)}) %collective-permute-start.1) | collective-permute-done | bytes 24608 | tf_op jit(solution)/shard_map/ppermute | solution.py:316
  77.9 1.9 %collective-permute-start.2 = (f32[48,128]{1,0:T(8,128)S(1)}, f32[48,128]{1,0:T(8,128)S(1)}, u32[]{:S(2)}, u32[]{:S(2)}) collective-permute-start(f32[48,128]{1,0:T(8,128)S(1)} %add.30), channel_id=1, source_target_pairs={{0,16},{4,20},{8,24},{12,28},{16,0},{20,4},{24,8},{28,12},{32,48},... | collective-permute-start | bytes 73736 | tf_op jit(solution)/shard_map/ppermute | solution.py:316
  79.8 5.3 %collective-permute-done.2 = f32[48,128]{1,0:T(8,128)S(1)} collective-permute-done((f32[48,128]{1,0:T(8,128)S(1)}, f32[48,128]{1,0:T(8,128)S(1)}, u32[]{:S(2)}, u32[]{:S(2)}) %collective-permute-start.2) | collective-permute-done | bytes 24608 | tf_op jit(solution)/shard_map/ppermute | solution.py:316
  85.1 1.9 %collective-permute-start.3 = (f32[48,128]{1,0:T(8,128)S(1)}, f32[48,128]{1,0:T(8,128)S(1)}, u32[]{:S(2)}, u32[]{:S(2)}) collective-permute-start(f32[48,128]{1,0:T(8,128)S(1)} %add.31), channel_id=1, source_target_pairs={{0,32},{4,36},{8,40},{12,44},{16,48},{20,52},{24,56},{28,60},{32,0... | collective-permute-start | bytes 73736 | tf_op jit(solution)/shard_map/ppermute | solution.py:316
  87.1 3.8 %collective-permute-done.3 = f32[48,128]{1,0:T(8,128)S(1)} collective-permute-done((f32[48,128]{1,0:T(8,128)S(1)}, f32[48,128]{1,0:T(8,128)S(1)}, u32[]{:S(2)}, u32[]{:S(2)}) %collective-permute-start.3) | collective-permute-done | bytes 24608 | tf_op jit(solution)/shard_map/ppermute | solution.py:316
  90.9 1.9 %collective-permute-start.4 = (f32[48,128]{1,0:T(8,128)S(1)}, f32[48,128]{1,0:T(8,128)S(1)}, u32[]{:S(2)}, u32[]{:S(2)}) collective-permute-start(f32[48,128]{1,0:T(8,128)S(1)} %add.32), channel_id=1, source_target_pairs={{0,64},{4,68},{8,72},{12,76},{16,80},{20,84},{24,88},{28,92},{32,9... | collective-permute-start | bytes 73736 | tf_op jit(solution)/shard_map/ppermute | solution.py:316
  92.8 4.7 %collective-permute-done.4 = f32[48,128]{1,0:T(8,128)S(1)} collective-permute-done((f32[48,128]{1,0:T(8,128)S(1)}, f32[48,128]{1,0:T(8,128)S(1)}, u32[]{:S(2)}, u32[]{:S(2)}) %collective-permute-start.4) | collective-permute-done | bytes 24608 | tf_op jit(solution)/shard_map/ppermute | solution.py:316
  97.5 5.1 %collective-permute-start.5 = (f32[48,128]{1,0:T(8,128)S(1)}, f32[48,128]{1,0:T(8,128)S(1)}, u32[]{:S(2)}, u32[]{:S(2)}) collective-permute-start(f32[48,128]{1,0:T(8,128)S(1)} %add.33), channel_id=1, source_target_pairs={{0,128},{4,132},{8,136},{12,140},{16,144},{20,148},{24,152},{28,15... | collective-permute-start | bytes 73736 | tf_op jit(solution)/shard_map/ppermute | solution.py:316
  102.6 4.5 %collective-permute-done.5 = f32[48,128]{1,0:T(8,128)S(1)} collective-permute-done((f32[48,128]{1,0:T(8,128)S(1)}, f32[48,128]{1,0:T(8,128)S(1)}, u32[]{:S(2)}, u32[]{:S(2)}) %collective-permute-start.5) | collective-permute-done | bytes 24608 | tf_op jit(solution)/shard_map/ppermute | solution.py:316
  107.1 11.5 %collective-permute-start.6 = (f32[48,128]{1,0:T(8,128)S(1)}, f32[48,128]{1,0:T(8,128)S(1)}, u32[]{:S(2)}, u32[]{:S(2)}) collective-permute-start(f32[48,128]{1,0:T(8,128)S(1)} %add.34), channel_id=1, source_target_pairs={{0,256},{4,260},{8,264},{12,268},{16,272},{20,276},{24,280},{28,28... | collective-permute-start | bytes 73736 | tf_op jit(solution)/shard_map/ppermute | solution.py:316
  118.6 3.0 %collective-permute-done.6 = f32[48,128]{1,0:T(8,128)S(1)} collective-permute-done((f32[48,128]{1,0:T(8,128)S(1)}, f32[48,128]{1,0:T(8,128)S(1)}, u32[]{:S(2)}, u32[]{:S(2)}) %collective-permute-start.6) | collective-permute-done | bytes 24608 | tf_op jit(solution)/shard_map/ppermute | solution.py:316
  121.5 1.9 %collective-permute-start.7 = (f32[48,128]{1,0:T(8,128)S(1)}, f32[48,128]{1,0:T(8,128)S(1)}, u32[]{:S(2)}, u32[]{:S(2)}) collective-permute-start(f32[48,128]{1,0:T(8,128)S(1)} %add.35), channel_id=1, source_target_pairs={{0,1},{1,0},{2,3},{3,2},{4,5},{5,4},{6,7},{7,6},{8,9},{9,8},{10,11... | collective-permute-start | bytes 73736 | tf_op jit(solution)/shard_map/ppermute | solution.py:319
  123.4 3.8 %collective-permute-done.7 = f32[48,128]{1,0:T(8,128)S(1)} collective-permute-done((f32[48,128]{1,0:T(8,128)S(1)}, f32[48,128]{1,0:T(8,128)S(1)}, u32[]{:S(2)}, u32[]{:S(2)}) %collective-permute-start.7) | collective-permute-done | bytes 24608 | tf_op jit(solution)/shard_map/ppermute | solution.py:319
  127.2 4.4 %collective-permute-start.8 = (f32[48,128]{1,0:T(8,128)S(1)}, f32[48,128]{1,0:T(8,128)S(1)}, u32[]{:S(2)}, u32[]{:S(2)}) collective-permute-start(f32[48,128]{1,0:T(8,128)S(1)} %add.36), channel_id=1, source_target_pairs={{0,2},{1,3},{2,0},{3,1},{4,6},{5,7},{6,4},{7,5},{8,10},{9,11},{10,... | collective-permute-start | bytes 73736 | tf_op jit(solution)/shard_map/ppermute | solution.py:319
  131.6 2.9 %collective-permute-done.8 = f32[48,128]{1,0:T(8,128)S(1)} collective-permute-done((f32[48,128]{1,0:T(8,128)S(1)}, f32[48,128]{1,0:T(8,128)S(1)}, u32[]{:S(2)}, u32[]{:S(2)}) %collective-permute-start.8) | collective-permute-done | bytes 24608 | tf_op jit(solution)/shard_map/ppermute | solution.py:319
  134.5 0.6 slice_bitcast_fusion
  135.0 0.1 fusion.2
  135.1 0.1 fusion.1
  135.2 0.6 fusion
  135.8 0.6 pad_maximum_fusion
  (8 shorter events, 0.0 us)
Async XLA Ops:
  64.3 3.3 %collective-permute-start = (f32[48,128]{1,0:T(8,128)}, f32[48,128]{1,0:T(8,128)S(1)}, u32[]{:S(2)}, u32[]{:S(2)}) collective-permute-start(f32[48,128]{1,0:T(8,128)} %get-tuple-element.8), channel_id=1, source_target_pairs={{0,4},{4,0},{8,12},{12,8},{16,20},{20,16},{24,28},{28,24},{32,36},... | collective-permute-start | bytes 73736 | tf_op jit(solution)/shard_map/ppermute | solution.py:316
  68.4 9.6 %collective-permute-start.1 = (f32[48,128]{1,0:T(8,128)S(1)}, f32[48,128]{1,0:T(8,128)S(1)}, u32[]{:S(2)}, u32[]{:S(2)}) collective-permute-start(f32[48,128]{1,0:T(8,128)S(1)} %add.29), channel_id=1, source_target_pairs={{0,8},{4,12},{8,0},{12,4},{16,24},{20,28},{24,16},{28,20},{32,40},... | collective-permute-start | bytes 73736 | tf_op jit(solution)/shard_map/ppermute | solution.py:316
  77.9 7.2 %collective-permute-start.2 = (f32[48,128]{1,0:T(8,128)S(1)}, f32[48,128]{1,0:T(8,128)S(1)}, u32[]{:S(2)}, u32[]{:S(2)}) collective-permute-start(f32[48,128]{1,0:T(8,128)S(1)} %add.30), channel_id=1, source_target_pairs={{0,16},{4,20},{8,24},{12,28},{16,0},{20,4},{24,8},{28,12},{32,48},... | collective-permute-start | bytes 73736 | tf_op jit(solution)/shard_map/ppermute | solution.py:316
  85.1 5.7 %collective-permute-start.3 = (f32[48,128]{1,0:T(8,128)S(1)}, f32[48,128]{1,0:T(8,128)S(1)}, u32[]{:S(2)}, u32[]{:S(2)}) collective-permute-start(f32[48,128]{1,0:T(8,128)S(1)} %add.31), channel_id=1, source_target_pairs={{0,32},{4,36},{8,40},{12,44},{16,48},{20,52},{24,56},{28,60},{32,0... | collective-permute-start | bytes 73736 | tf_op jit(solution)/shard_map/ppermute | solution.py:316
  90.9 6.6 %collective-permute-start.4 = (f32[48,128]{1,0:T(8,128)S(1)}, f32[48,128]{1,0:T(8,128)S(1)}, u32[]{:S(2)}, u32[]{:S(2)}) collective-permute-start(f32[48,128]{1,0:T(8,128)S(1)} %add.32), channel_id=1, source_target_pairs={{0,64},{4,68},{8,72},{12,76},{16,80},{20,84},{24,88},{28,92},{32,9... | collective-permute-start | bytes 73736 | tf_op jit(solution)/shard_map/ppermute | solution.py:316
  97.5 9.6 %collective-permute-start.5 = (f32[48,128]{1,0:T(8,128)S(1)}, f32[48,128]{1,0:T(8,128)S(1)}, u32[]{:S(2)}, u32[]{:S(2)}) collective-permute-start(f32[48,128]{1,0:T(8,128)S(1)} %add.33), channel_id=1, source_target_pairs={{0,128},{4,132},{8,136},{12,140},{16,144},{20,148},{24,152},{28,15... | collective-permute-start | bytes 73736 | tf_op jit(solution)/shard_map/ppermute | solution.py:316
  107.1 14.4 %collective-permute-start.6 = (f32[48,128]{1,0:T(8,128)S(1)}, f32[48,128]{1,0:T(8,128)S(1)}, u32[]{:S(2)}, u32[]{:S(2)}) collective-permute-start(f32[48,128]{1,0:T(8,128)S(1)} %add.34), channel_id=1, source_target_pairs={{0,256},{4,260},{8,264},{12,268},{16,272},{20,276},{24,280},{28,28... | collective-permute-start | bytes 73736 | tf_op jit(solution)/shard_map/ppermute | solution.py:316
  121.5 5.7 %collective-permute-start.7 = (f32[48,128]{1,0:T(8,128)S(1)}, f32[48,128]{1,0:T(8,128)S(1)}, u32[]{:S(2)}, u32[]{:S(2)}) collective-permute-start(f32[48,128]{1,0:T(8,128)S(1)} %add.35), channel_id=1, source_target_pairs={{0,1},{1,0},{2,3},{3,2},{4,5},{5,4},{6,7},{7,6},{8,9},{9,8},{10,11... | collective-permute-start | bytes 73736 | tf_op jit(solution)/shard_map/ppermute | solution.py:319
  127.2 7.2 %collective-permute-start.8 = (f32[48,128]{1,0:T(8,128)S(1)}, f32[48,128]{1,0:T(8,128)S(1)}, u32[]{:S(2)}, u32[]{:S(2)}) collective-permute-start(f32[48,128]{1,0:T(8,128)S(1)} %add.36), channel_id=1, source_target_pairs={{0,2},{1,3},{2,0},{3,1},{4,6},{5,7},{6,4},{7,5},{8,10},{9,11},{10,... | collective-permute-start | bytes 73736 | tf_op jit(solution)/shard_map/ppermute | solution.py:319

commit v2 on v1

v2 whole, which is shorter than its diff:
```python
import jax
import jax.numpy as jnp
from jax import lax
from jax.experimental import pallas as pl
from jax.experimental.pallas import tpu as pltpu
from jax.sharding import PartitionSpec as P

POS = 221
CH = 8
R = 128
F = 64
OWN = 4
SITES = 1024
HALF = 112
GROUP = 8
CHUNKS = HALF // GROUP
XPOS = 2 * HALF + 2
WIN = SITES + 8
SPARE = OWN * CHUNKS

SAMP = ("z_high", "z_low", "x", "core")

F32 = jnp.float32
BF = jnp.bfloat16
NT = (((1,), (1,)), ((), ()))


def mm(a, b):
    return jnp.dot(a, b, preferred_element_type=F32)


def mm_nt(a, b):
    return lax.dot_general(a, b, NT, preferred_element_type=F32)


def split2(v):
    hi = v.astype(BF)
    return hi, (v - hi.astype(F32)).astype(BF)


def halves(v):
    zero = jnp.zeros((8, R), v.dtype)
    left = jnp.concatenate([v[:, :R], zero], axis=1)
    right = jnp.concatenate([zero, v[:, R:]], axis=1)
    return jnp.concatenate([left, right], axis=0)


def pooling_kernel(
    dev, counts, reads, starts, x_hbm, conv_w, bias, mix, query, cot,
    pooled, grads,
    x, hid, feat, slope, weight_rows, gate_rows, query_rows,
    hid_0, hid_1, feat_0, feat_1, score_0, score_1, second_0, second_1, relu_0, relu_1,
    w_num, w_den, d_num, d_den, acc_mix, acc_conv, acc_query, sems,
):
    me = dev[0]
    count = counts[0, me]
    total = count * CHUNKS
    hid_ring = (hid_0, hid_1)
    feat_ring, score_ring = (feat_0, feat_1), (score_0, score_1)
    second_ring, relu_ring = (second_0, second_1), (relu_0, relu_1)

    copies = [
        pltpu.make_async_copy(x_hbm.at[0, s], x.at[s, pl.ds(1, POS)], sems.at[s])
        for s in range(OWN)
    ]
    for copy in copies:
        copy.start()
    for s in range(OWN):
        x[s, 0] = jnp.zeros((CH, R), BF)
        x[s, POS + 1 :] = jnp.zeros((XPOS - POS - 1, CH, R), BF)

    zeros = lambda *s: jnp.zeros(s, F32)
    cw = conv_w[...].astype(F32)
    b = bias[...]
    b_hi = b.astype(BF).astype(F32)
    b_mid = (b - b_hi).astype(BF).astype(F32)
    b_lo = b - b_hi - b_mid
    b_rows = jnp.concatenate([b_hi, b_mid, b_lo, zeros(13, F)], axis=0)
    even = jnp.concatenate([cw, zeros(8, F), b_rows, zeros(80, F)], axis=0)
    odd = jnp.concatenate([zeros(8, F), cw, b_rows, zeros(80, F)], axis=0)
    conv_lhs = jnp.concatenate([even.T, odd.T], axis=0)[:, :48].astype(BF)
    pad_mix = jnp.concatenate([mix[...].astype(F32), zeros(64, F)], axis=0)
    mix_t = (0.5 * pad_mix.T[:, :F]).astype(BF)
    mix_b = mix[...]
    q = 0.5 * query[...]
    q_hi = q.astype(BF).astype(F32)
    q_lo = q - q_hi
    query_lhs = jnp.concatenate(
        [jnp.broadcast_to(q_hi, (8, F)), jnp.broadcast_to(q_lo, (8, F))], axis=0
    ).astype(BF)
    query_rows[...] = jnp.concatenate([jnp.broadcast_to(q, (128, F)), zeros(128, F)], axis=1).T[:F]
    ones = jnp.ones((16, 2 * R), BF)
    row8 = lax.broadcasted_iota(jnp.int32, (8, 2 * R), 0)
    lane8 = lax.broadcasted_iota(jnp.int32, (8, 2 * R), 1)
    row16 = lax.broadcasted_iota(jnp.int32, (16, F), 0) % GROUP

    def place(k):
        slot = jnp.int32(0)
        for s in range(1, OWN):
            slot = slot + (k >= s * CHUNKS).astype(jnp.int32)
        return slot, k - slot * CHUNKS

    def window(slot, c, i):
        at = c * GROUP + 2 * i
        left = x[slot, pl.ds(at, 4)].reshape(32, R)
        right = x[slot, pl.ds(at + HALF, 4)].reshape(32, R)
        return jnp.concatenate([jnp.concatenate([left, right], axis=1), ones], axis=0)

    w_num[...] = jnp.zeros(w_num.shape, F32)
    w_den[...] = jnp.zeros(w_den.shape, F32)
    for copy in copies:
        copy.wait()

    def first_dots(k, half, i):
        slot, c = place(jnp.minimum(k, SPARE - 1))
        pre = mm(conv_lhs, window(slot, c, i)).astype(BF)
        rows = slice(128 * i, 128 * i + 128)
        relu = jnp.maximum(pre, jnp.zeros_like(pre))
        hid[k, rows, :] = relu
        hid_ring[half][rows, :] = relu

    def second_dots(half):
        return [mm(mix_t, hid_ring[half][F * j : F * j + F, :]) for j in range(GROUP)]

    def second_rest(k, dots):
        for j, h in enumerate(dots):
            rows = slice(F * j, F * j + F)
            a = 1.0 + jnp.tanh(h)
            f = h * a
            feat[k, rows, :] = f.astype(BF)
            slope[k, rows, :] = (a * (1.0 + ((h + h) - f))).astype(BF)

    def score_stage(k, half):
        slot, c = place(k)
        score = jnp.zeros((8, 2 * R), F32)
        for j in range(GROUP):
            s = mm(query_lhs, feat_ring[half][F * j : F * j + F, :])
            score = jnp.where(row8 == j, s[:8] + s[8:], score)
        opening = 0.5 + 0.5 * jnp.tanh(score)
        read = jnp.where(lane8 < R, lane8, lane8 - R)
        position = jnp.where(lane8 < R, row8, row8 + HALF) + GROUP * c
        live = (read < reads[0, me * OWN + slot]) & (position < POS)
        weight = jnp.where(live, opening, 0.0)
        weight_rows[k] = weight
        gate_rows[k] = weight * (1.0 - opening)
        return weight

    def pool_dot(half, lhs, num, j):
        n = mm_nt(lhs, feat_ring[half][F * j : F * j + F, :])
        return jnp.where(row16 == j, n, num)

    def pool_rest(k, weight, num, valid):
        slot, c = place(k)
        den_l = jnp.sum(weight[:, :R], axis=1, keepdims=True)
        den_r = jnp.sum(weight[:, R:], axis=1, keepdims=True)
        first = starts[0, me * OWN + slot] + GROUP * c
        for part, den, at in ((num[:8], den_l, first), (num[8:], den_r, first + HALF)):
            here = pl.ds(at, 8)
            w_num[here, :] += jnp.where(valid, part, 0.0)
            w_den[here, :] += jnp.where(valid, jnp.broadcast_to(den, (8, 128)), 0.0)

    @pl.loop(0, total // 2 + 2)
    def _(i):
        new = [jnp.minimum(2 * i + half, SPARE) for half in range(2)]
        mid = [jnp.clip(2 * i + half - 2, 0, SPARE) for half in range(2)]
        old = [jnp.maximum(2 * i + half - 4, 0) for half in range(2)]
        dots_0 = second_dots(0)
        weights = [score_stage(old[half], half) for half in range(2)]
        dots_1 = second_dots(1)
        second_rest(mid[0], dots_0)
        for n in range(GROUP // 2):
            first_dots(new[0], 0, n)
        second_rest(mid[1], dots_1)
        lhs = [halves(w).astype(BF) for w in weights]
        nums = [jnp.zeros((16, F), F32)] * 2
        for n in range(GROUP // 2):
            first_dots(new[1], 1, n)
            for half in range(2):
                for j in (2 * n, 2 * n + 1):
                    nums[half] = pool_dot(half, lhs[half], nums[half], j)
        for half in range(2):
            pool_rest(old[half], weights[half], nums[half], i >= 2)
            feat_ring[half][...] = feat[mid[half]]

    d_num[SITES:, :] = jnp.zeros((WIN - SITES, 128), F32)
    d_den[SITES:, :] = jnp.zeros((WIN - SITES, 128), F32)
    for i in range(SITES // 128):
        here = slice(128 * i, 128 * i + 128)
        num = w_num[here, :]
        den = w_den[here, :]
        inv = 1.0 / jnp.maximum(den, 1.0)
        out = jnp.concatenate([num * inv[:, :F], jnp.zeros((128, F), F32)], axis=1)
        pooled[:, here] = out.T[:F]
        cot_t = jnp.concatenate([cot[:, here], jnp.zeros((F, 128), F32)], axis=0).T
        dn = cot_t * inv
        d_num[here, :] = dn
        inner = jnp.sum(dn[:, :F] * num, axis=1, keepdims=True)
        d_den[here, :] = jnp.where(den > 1.0, -(jnp.broadcast_to(inner, (128, 128)) * inv), 0.0)

    acc_mix[...] = jnp.zeros(acc_mix.shape, F32)
    acc_conv[...] = jnp.zeros(acc_conv.shape, F32)
    acc_query[...] = jnp.zeros(acc_query.shape, F32)

    def cut(k):
        slot, c = place(k)
        first = starts[0, me * OWN + slot] + GROUP * c
        return first, jnp.concatenate(
            [d_num[pl.ds(first, 8), :], d_num[pl.ds(first + HALF, 8), :]], axis=0
        )

    def weight_dot(lhs, k, d_weight, j):
        w = mm(lhs, feat[k, F * j : F * j + F, :])
        w = jnp.concatenate([w[:8, :R] + w[16:24, :R], w[8:16, R:] + w[24:, R:]], axis=1)
        return jnp.where(row8 == j, w, d_weight)

    def second_back(k, half, valid):
        _, dn = cut(k)
        turned = jnp.concatenate([0.5 * dn, zeros(112, 128)], axis=0).T[:F]
        q = query_rows[...]
        sums = zeros(F, R)
        for j in range(GROUP):
            rows = slice(F * j, F * j + F)
            f = feat[k, rows, :].astype(F32)
            e = slope[k, rows, :].astype(F32)
            out = []
            for side in range(2):
                lanes = slice(R * side, R * side + R)
                at = GROUP * side + j
                w = weight_rows[k, j : j + 1, lanes]
                s = score_ring[half][j : j + 1, lanes]
                d_feat = turned[:, at : at + 1] * w + q * s
                out.append((d_feat * e[:, lanes]).astype(BF))
                sums = sums + f[:, lanes] * s
            second_ring[half][rows, :] = jnp.concatenate(out, axis=1)
        acc_query[...] += jnp.where(valid, sums, 0.0)

    @pl.loop(0, total // 2 + 3)
    def _(i):
        inside = lambda v: (v >= 0) & (v < total)
        bound = lambda v: jnp.clip(v, 0, SPARE - 1)
        for half in range(2):
            k0, k1, k2, k3 = (2 * i + half - 2 * lag for lag in range(4))
            new, old, last = bound(k0), bound(k2), bound(k3)
            slot, c = place(last)
            first, dn = cut(new)
            hi, lo = split2(dn[:, :F])
            lhs = jnp.concatenate([hi, lo], axis=0)
            d_weight = jnp.zeros((8, 2 * R), F32)
            g_conv = zeros(48, 128)
            g_mix = zeros(F, F)
            for n in range(GROUP // 2):
                both = slice(128 * n, 128 * n + 128)
                g_conv += mm_nt(window(slot, c, n), relu_ring[half][both, :])
                h = [hid[old, F * j : F * j + F, :] for j in (2 * n, 2 * n + 1)]
                d2 = [second_ring[half][F * j : F * j + F, :] for j in (2 * n, 2 * n + 1)]
                for j in range(2):
                    dh = mm(mix_b, d2[j]).astype(BF)
                    at = F * (2 * n + j)
                    relu_ring[half][at : at + F, :] = jnp.where(h[j] > 0, dh, jnp.zeros_like(dh))
                g_mix += mm_nt(jnp.concatenate(h, axis=1), jnp.concatenate(d2, axis=1))
                for j in (2 * n, 2 * n + 1):
                    d_weight = weight_dot(lhs, new, d_weight, j)
            second_back(bound(k1), half, inside(k1))
            acc_conv[...] += jnp.where(inside(k3), g_conv, 0.0)
            acc_mix[...] += jnp.where(inside(k2), g_mix, 0.0)
            dd = jnp.concatenate(
                [d_den[pl.ds(first, 8), :], d_den[pl.ds(first + HALF, 8), :]], axis=1
            )
            score_ring[half][...] = (d_weight + dd) * gate_rows[new]

    turned = acc_conv[...]
    g_conv = turned[0:24, :F] + turned[8:32, F:]
    g_bias = turned[32:33, :F] + turned[32:33, F:]
    ones_f = jnp.concatenate([acc_query[...], zeros(F, R)], axis=0).T
    g_query = jnp.sum(ones_f, axis=0, keepdims=True)[:, :F]
    rest = jnp.concatenate([g_conv, g_bias, g_query, zeros(6, F)], axis=0)
    gm = acc_mix[...]
    grads[0:32, :] = jnp.concatenate([gm[:32], gm[32:]], axis=1)
    grads[32:48, :] = jnp.concatenate([rest[:16], rest[16:]], axis=1)


def run_kernel(dev, counts, reads, starts, x, conv_w, bias, mix, query, cot, interpret=False):
    smem = pl.BlockSpec(memory_space=pltpu.SMEM)
    vmem = pl.BlockSpec(memory_space=pltpu.VMEM)
    big = (SPARE + 1, GROUP * F, 2 * R)
    return pl.pallas_call(
        pooling_kernel,
        out_shape=(
            jax.ShapeDtypeStruct((F, SITES), F32),
            jax.ShapeDtypeStruct((48, 128), F32),
        ),
        in_specs=[smem] * 4 + [pl.BlockSpec(memory_space=pl.ANY)] + [vmem] * 5,
        out_specs=(vmem, vmem),
        scratch_shapes=[
            pltpu.VMEM((OWN, XPOS, CH, R), BF),
            pltpu.VMEM(big, BF),
            pltpu.VMEM(big, BF),
            pltpu.VMEM(big, BF),
            pltpu.VMEM((SPARE + 1, 8, 2 * R), F32),
            pltpu.VMEM((SPARE + 1, 8, 2 * R), F32),
            pltpu.VMEM((F, R), F32),
            pltpu.VMEM(big[1:], BF),
            pltpu.VMEM(big[1:], BF),
            pltpu.VMEM(big[1:], BF),
            pltpu.VMEM(big[1:], BF),
            pltpu.VMEM((8, 2 * R), F32),
            pltpu.VMEM((8, 2 * R), F32),
            pltpu.VMEM(big[1:], BF),
            pltpu.VMEM(big[1:], BF),
            pltpu.VMEM(big[1:], BF),
            pltpu.VMEM(big[1:], BF),
            pltpu.VMEM((WIN, F), F32),
            pltpu.VMEM((WIN, 128), F32),
            pltpu.VMEM((WIN, 128), F32),
            pltpu.VMEM((WIN, 128), F32),
            pltpu.VMEM((F, F), F32),
            pltpu.VMEM((48, 128), F32),
            pltpu.VMEM((F, R), F32),
            pltpu.SemaphoreType.DMA((OWN,)),
        ],
        compiler_params=pltpu.CompilerParams(vmem_limit_bytes=60 * 2**20),
        interpret=interpret,
    )(dev, counts, reads, starts, x, conv_w, bias, mix, query, cot)


def on_device(
    read_blocks, block_counts, block_reads, block_starts,
    conv_weight, conv_bias, mix_weight, pool_query, site_cotangent,
):
    dev = lax.axis_index(SAMP).astype(jnp.int32).reshape(1)
    pooled, grads = run_kernel(
        dev, block_counts, block_reads, block_starts,
        read_blocks,
        conv_weight.reshape(3 * CH, F), conv_bias.reshape(1, F), mix_weight,
        pool_query.reshape(1, F), site_cotangent[0, 0],
    )
    for axes, size in ((("x", "core"), 8), (("z_low", "rep"), 8), ("z_high", 8)):
        every = jnp.broadcast_to(grads, (size, *grads.shape))
        grads = jnp.sum(lax.all_to_all(every, axes, 0, 0), axis=0)
    g_mix = jnp.concatenate([grads[:32, :F], grads[:32, F:]], axis=0)
    rest = jnp.concatenate([grads[32:, :F], grads[32:, F:]], axis=0)
    return (pooled[None, None], rest[:24].reshape(3, CH, F), rest[24], g_mix, rest[25])


def solution(mesh):
    split = jax.sharding.Mesh(
        mesh.devices.reshape(8, 2, 4, 2, mesh.shape["rep"]), SAMP + ("rep",)
    )
    in_specs = (
        P("rep", SAMP, None, None, None),
        P("rep", None),
        P("rep", None),
        P("rep", None),
        P(),
        P(),
        P(),
        P(),
        P("rep", SAMP, None, None),
    )
    out_specs = (P("rep", SAMP, None, None), P(), P(), P(), P())
    return jax.shard_map(
        on_device, mesh=split, in_specs=in_specs, out_specs=out_specs, check_vma=False
    )
```

time: 137 us -> 107 us (0.78)
  blocking collectives: 0 us -> 85.1 us
  Pallas kernels: 60.8 us -> 18.5 us
  starting transfers between devices: 38.3 us -> 0 us
  waiting for transfers between devices: 31 us -> 0 us
  local copies, waits for them, and re-layouts: 3.62 us -> 1.51 us
    all_to_all x0 -> x3, blocking collectives: none -> 85.1 us  [on_device(): grads = jnp.sum(lax.all_to_all(every, axes, 0, 0), axis=0)]
    pallas_call x1, Pallas kernels: 60.8 us -> 18.5 us  [run_kernel(): pl.pallas_call(pooling_kernel, out_shape=(jax.ShapeDtypeStruct((F, SITES)...]
    ppermute x9 -> x0, starting transfers between devices: 38.3 us -> none  [the longest x7 32 us: on_device(): lax.ppermute(grads, 'samp', [(i, i ^ stride) for i in range(128)])]
    ppermute x9 -> x0, waiting for transfers between devices: 31 us -> none  [the longest x7 24.4 us: on_device(): lax.ppermute(grads, 'samp', [(i, i ^ stride) for i in range(128)])]
    reshape x1 -> x0, local copies, waits for them, and re-layouts: 2.89 us -> none  [pad_blocks(): return padded.reshape(OWN, XPOS * CH, R)]
  transfers between devices with their start and end apart: 9 -> 0, of which waited for: 9 -> 0; matrix products, arithmetic and copies ran while one was open for 0% -> 0% of each run, Pallas kernels for 0% -> 0%
where the time goes in v2:
time: 107 us
  blocking collectives  85.1 us (80%)
  Pallas kernels  18.5 us (17%)
  local copies, waits for them, and re-layouts  1.51 us (1%)
  other arithmetic  1.27 us (1%)
    all_to_all x3, blocking collectives, on_device(): grads = jnp.sum(lax.all_to_all(every, axes, 0, 0), axis=0)  85.1 us
    pallas_call x1, Pallas kernels, run_kernel(): pl.pallas_call(pooling_kernel, out_shape=(jax.ShapeDtypeStruct((F, SITES)...  18.5 us

profile of v2, /device:TPU:2, one launch (start us, length us, event | category | flops | bytes accessed | tf_op | source)
XLA Modules:
  0.0 107.1 jit_solution(15151846774788652572)
XLA Ops:
  0.6 18.5 %shard_map.128 = (f32[64,1024]{1,0:T(8,128)}, f32[48,128]{1,0:T(8,128)}) custom-call(s32[1]{0:T(128)} %bitcast.dev, s32[1,128]{1,0:T(1,128)} %counts.1, s32[1,512]{1,0:T(1,128)} %reads.1, s32[1,512]{1,0:T(1,128)} %starts.1, bf16[1,4,221,8,128]{4,3,2,1,0:T(8,128)(2,1)} %x_hbm.1, bf16[24,64]{1,0:T(8,128)(2,1)} %bitcast.13, f32[1,64]{1,0:T(1,128)} %bitcast.14, ...), custom_call_target="tpu_custom_call" | custom-call | tf_op jit(solution)/shard_map/pallas_call | solution.py:286
  19.1 0.8 broadcast_in_dim.13
  19.9 41.9 %all_to_all.15 = f32[8,48,128]{2,1,0:T(8,128)S(1)} all-to-all(f32[8,48,128]{2,1,0:T(8,128)S(1)} %broadcast_in_dim.13), channel_id=1, replica_groups=mesh['z_high'=8,'z_low'=2,'x'=4,'core'=2,'rep'=4] {'x','core'}, dimensions={0} | all-to-all | bytes 393216 | tf_op jit(solution)/shard_map/all_to_all | solution.py:339
  61.9 12.8 %all_to_all.16 = f32[8,48,128]{2,1,0:T(8,128)S(1)} all-to-all(f32[8,48,128]{2,1,0:T(8,128)S(1)} %broadcast_in_dim.14), channel_id=1, replica_groups=mesh['z_high'=8,'z_low'=2,'x'=4,'core'=2,'rep'=4] {'z_low','rep'}, dimensions={0} | all-to-all | bytes 393216 | tf_op jit(solution)/shard_map/all_to_all | solution.py:339
  74.7 30.4 %all_to_all.17 = f32[8,48,128]{2,1,0:T(8,128)S(1)} all-to-all(f32[8,48,128]{2,1,0:T(8,128)S(1)} %broadcast_in_dim.15), channel_id=1, replica_groups=mesh['z_high'=8,'z_low'=2,'x'=4,'core'=2,'rep'=4] {'z_high'}, dimensions={0} | all-to-all | bytes 393216 | tf_op jit(solution)/shard_map/all_to_all | solution.py:339
  105.1 0.6 slice_bitcast_fusion
  105.7 0.1 fusion.2
  105.8 0.1 fusion.1
  105.9 0.6 fusion
  106.5 0.6 pad_maximum_fusion
  (5 shorter events, 0.1 us)

commit v3 on v2

--- a/solution.py
+++ b/solution.py
@@ -17,6 +17,7 @@
 XPOS = 2 * HALF + 2
 WIN = SITES + 8
 SPARE = OWN * CHUNKS
+STEP = 4
 
 SAMP = ("z_high", "z_low", "x", "core")
 
@@ -36,6 +37,15 @@
 def split2(v):
     hi = v.astype(BF)
     return hi, (v - hi.astype(F32)).astype(BF)
+
+
+def spread(v):
+    twice = jnp.concatenate([v, v], axis=1)
+    row = lax.broadcasted_iota(jnp.int32, twice.shape, 0) % GROUP
+    late = lax.broadcasted_iota(jnp.int32, twice.shape, 1) // F
+    return jnp.concatenate(
+        [jnp.where(row == 2 * m + late, twice, 0.0) for m in range(GROUP // 2)], axis=1
+    )
 
 
 def halves(v):
@@ -49,15 +59,14 @@
     dev, counts, reads, starts, x_hbm, conv_w, bias, mix, query, cot,
     pooled, grads,
     x, hid, feat, slope, weight_rows, gate_rows, query_rows,
-    hid_0, hid_1, feat_0, feat_1, score_0, score_1, second_0, second_1, relu_0, relu_1,
-    w_num, w_den, d_num, d_den, acc_mix, acc_conv, acc_query, sems,
+    w_num, w_den, d_num, d_den, acc_mix, acc_conv, acc_query, sems, *rings,
 ):
     me = dev[0]
     count = counts[0, me]
     total = count * CHUNKS
-    hid_ring = (hid_0, hid_1)
-    feat_ring, score_ring = (feat_0, feat_1), (score_0, score_1)
-    second_ring, relu_ring = (second_0, second_1), (relu_0, relu_1)
+    hid_ring, feat_ring, second_ring, relu_ring, score_ring, turned_ring = (
+        rings[STEP * n : STEP * n + STEP] for n in range(6)
+    )
 
     copies = [
         pltpu.make_async_copy(x_hbm.at[0, s], x.at[s, pl.ds(1, POS)], sems.at[s])
@@ -85,14 +94,15 @@
     q = 0.5 * query[...]
     q_hi = q.astype(BF).astype(F32)
     q_lo = q - q_hi
-    query_lhs = jnp.concatenate(
-        [jnp.broadcast_to(q_hi, (8, F)), jnp.broadcast_to(q_lo, (8, F))], axis=0
+    query_lhs = spread(
+        jnp.concatenate([jnp.broadcast_to(q_hi, (8, F)), jnp.broadcast_to(q_lo, (8, F))], axis=0)
     ).astype(BF)
     query_rows[...] = jnp.concatenate([jnp.broadcast_to(q, (128, F)), zeros(128, F)], axis=1).T[:F]
     ones = jnp.ones((16, 2 * R), BF)
     row8 = lax.broadcasted_iota(jnp.int32, (8, 2 * R), 0)
     lane8 = lax.broadcasted_iota(jnp.int32, (8, 2 * R), 1)
-    row16 = lax.broadcasted_iota(jnp.int32, (16, F), 0) % GROUP
+    row16 = lax.broadcasted_iota(jnp.int32, (16, 128), 0) % GROUP
+    pair16 = row16 // 2
 
     def place(k):
         slot = jnp.int32(0)
@@ -125,17 +135,16 @@
     def second_rest(k, dots):
         for j, h in enumerate(dots):
             rows = slice(F * j, F * j + F)
-            a = 1.0 + jnp.tanh(h)
+            t = jnp.tanh(h)
+            a = 1.0 + t
             f = h * a
             feat[k, rows, :] = f.astype(BF)
-            slope[k, rows, :] = (a * (1.0 + ((h + h) - f))).astype(BF)
+            slope[k, rows, :] = (a + f * (1.0 - t)).astype(BF)
 
     def score_stage(k, half):
         slot, c = place(k)
-        score = jnp.zeros((8, 2 * R), F32)
-        for j in range(GROUP):
-            s = mm(query_lhs, feat_ring[half][F * j : F * j + F, :])
-            score = jnp.where(row8 == j, s[:8] + s[8:], score)
+        score = mm(query_lhs, feat_ring[half][...])
+        score = score[:8] + score[8:]
         opening = 0.5 + 0.5 * jnp.tanh(score)
         read = jnp.where(lane8 < R, lane8, lane8 - R)
         position = jnp.where(lane8 < R, row8, row8 + HALF) + GROUP * c
@@ -143,44 +152,70 @@
         weight = jnp.where(live, opening, 0.0)
         weight_rows[k] = weight
         gate_rows[k] = weight * (1.0 - opening)
-        return weight
-
-    def pool_dot(half, lhs, num, j):
-        n = mm_nt(lhs, feat_ring[half][F * j : F * j + F, :])
-        return jnp.where(row16 == j, n, num)
-
-    def pool_rest(k, weight, num, valid):
+        dens = [
+            jnp.broadcast_to(jnp.sum(weight[:, at : at + R], axis=1, keepdims=True), (8, 128))
+            for at in (0, R)
+        ]
+        return halves(weight).astype(BF), dens
+
+    def pool_dot(half, lhs, num, n):
+        part = mm_nt(lhs, feat_ring[half][256 * n : 256 * n + 256, :])
+        for m in range(2):
+            num = jnp.where(pair16 == 2 * n + m, part[:, 128 * m : 128 * m + 128], num)
+        return num
+
+    def pool_rest(k, dens, num, valid):
         slot, c = place(k)
-        den_l = jnp.sum(weight[:, :R], axis=1, keepdims=True)
-        den_r = jnp.sum(weight[:, R:], axis=1, keepdims=True)
         first = starts[0, me * OWN + slot] + GROUP * c
-        for part, den, at in ((num[:8], den_l, first), (num[8:], den_r, first + HALF)):
+        num = jnp.where(row16 % 2 == 0, num, pltpu.roll(num, F, 1))[:, :F]
+        for part, den, at in ((num[:8], dens[0], first), (num[8:], dens[1], first + HALF)):
             here = pl.ds(at, 8)
             w_num[here, :] += jnp.where(valid, part, 0.0)
-            w_den[here, :] += jnp.where(valid, jnp.broadcast_to(den, (8, 128)), 0.0)
-
-    @pl.loop(0, total // 2 + 2)
+            w_den[here, :] += jnp.where(valid, den, 0.0)
+
+    inside = lambda v: (v >= 0) & (v < total)
+    bound = lambda v: jnp.clip(v, 0, SPARE - 1)
+    steps = (total + STEP - 1) // STEP
+
+    def forward_step(i, stages):
+        first, second, pool = (n in stages for n in range(3))
+        chunks = range(STEP)
+        new = [jnp.minimum(STEP * i + n, SPARE) for n in chunks]
+        mid = [jnp.clip(STEP * (i - 1) + n, 0, SPARE) for n in chunks]
+        old = [bound(STEP * (i - 2) + n) for n in chunks]
+        nums = [jnp.zeros((16, 128), F32)] * STEP
+        dots, weights = {}, {}
+        if second:
+            dots[0] = second_dots(0)
+        if pool:
+            weights = {n: score_stage(old[n], n) for n in chunks}
+        for n in chunks:
+            if second:
+                if n + 1 < STEP:
+                    dots[n + 1] = second_dots(n + 1)
+                second_rest(mid[n], dots.pop(n))
+            todo = (2 * n - 2, 2 * n - 1) if pool and n in (1, 2) else ()
+            for m in range(GROUP // 2):
+                if first:
+                    first_dots(new[n], n, m)
+                if m % 2:
+                    for t in todo:
+                        nums[t] = pool_dot(t, weights[t][0], nums[t], m // 2)
+            for t in todo:
+                pool_rest(old[t], weights[t][1], nums[t], inside(STEP * (i - 2) + t))
+        if second:
+            for n in chunks:
+                feat_ring[n][...] = feat[mid[n]]
+
+    forward_step(0, (0,))
+    forward_step(1, (0, 1))
+
+    @pl.loop(2, steps)
     def _(i):
-        new = [jnp.minimum(2 * i + half, SPARE) for half in range(2)]
-        mid = [jnp.clip(2 * i + half - 2, 0, SPARE) for half in range(2)]
-        old = [jnp.maximum(2 * i + half - 4, 0) for half in range(2)]
-        dots_0 = second_dots(0)
-        weights = [score_stage(old[half], half) for half in range(2)]
-        dots_1 = second_dots(1)
-        second_rest(mid[0], dots_0)
-        for n in range(GROUP // 2):
-            first_dots(new[0], 0, n)
-        second_rest(mid[1], dots_1)
-        lhs = [halves(w).astype(BF) for w in weights]
-        nums = [jnp.zeros((16, F), F32)] * 2
-        for n in range(GROUP // 2):
-            first_dots(new[1], 1, n)
-            for half in range(2):
-                for j in (2 * n, 2 * n + 1):
-                    nums[half] = pool_dot(half, lhs[half], nums[half], j)
-        for half in range(2):
-            pool_rest(old[half], weights[half], nums[half], i >= 2)
-            feat_ring[half][...] = feat[mid[half]]
+        forward_step(i, (0, 1, 2))
+
+    forward_step(steps, (1, 2))
+    forward_step(steps + 1, (2,))
 
     d_num[SITES:, :] = jnp.zeros((WIN - SITES, 128), F32)
     d_den[SITES:, :] = jnp.zeros((WIN - SITES, 128), F32)
@@ -208,14 +243,8 @@
             [d_num[pl.ds(first, 8), :], d_num[pl.ds(first + HALF, 8), :]], axis=0
         )
 
-    def weight_dot(lhs, k, d_weight, j):
-        w = mm(lhs, feat[k, F * j : F * j + F, :])
-        w = jnp.concatenate([w[:8, :R] + w[16:24, :R], w[8:16, R:] + w[24:, R:]], axis=1)
-        return jnp.where(row8 == j, w, d_weight)
-
     def second_back(k, half, valid):
-        _, dn = cut(k)
-        turned = jnp.concatenate([0.5 * dn, zeros(112, 128)], axis=0).T[:F]
+        turned = turned_ring[half][...]
         q = query_rows[...]
         sums = zeros(F, R)
         for j in range(GROUP):
@@ -234,39 +263,58 @@
             second_ring[half][rows, :] = jnp.concatenate(out, axis=1)
         acc_query[...] += jnp.where(valid, sums, 0.0)
 
-    @pl.loop(0, total // 2 + 3)
-    def _(i):
-        inside = lambda v: (v >= 0) & (v < total)
-        bound = lambda v: jnp.clip(v, 0, SPARE - 1)
-        for half in range(2):
-            k0, k1, k2, k3 = (2 * i + half - 2 * lag for lag in range(4))
+    def backward_step(i, stages):
+        weight, second, relu, conv = (n in stages for n in range(4))
+        for half in range(STEP):
+            k0, k1, k2, k3 = (STEP * (i - lag) + half for lag in range(4))
             new, old, last = bound(k0), bound(k2), bound(k3)
             slot, c = place(last)
-            first, dn = cut(new)
-            hi, lo = split2(dn[:, :F])
-            lhs = jnp.concatenate([hi, lo], axis=0)
-            d_weight = jnp.zeros((8, 2 * R), F32)
             g_conv = zeros(48, 128)
             g_mix = zeros(F, F)
             for n in range(GROUP // 2):
                 both = slice(128 * n, 128 * n + 128)
-                g_conv += mm_nt(window(slot, c, n), relu_ring[half][both, :])
-                h = [hid[old, F * j : F * j + F, :] for j in (2 * n, 2 * n + 1)]
-                d2 = [second_ring[half][F * j : F * j + F, :] for j in (2 * n, 2 * n + 1)]
-                for j in range(2):
-                    dh = mm(mix_b, d2[j]).astype(BF)
-                    at = F * (2 * n + j)
-                    relu_ring[half][at : at + F, :] = jnp.where(h[j] > 0, dh, jnp.zeros_like(dh))
-                g_mix += mm_nt(jnp.concatenate(h, axis=1), jnp.concatenate(d2, axis=1))
-                for j in (2 * n, 2 * n + 1):
-                    d_weight = weight_dot(lhs, new, d_weight, j)
-            second_back(bound(k1), half, inside(k1))
-            acc_conv[...] += jnp.where(inside(k3), g_conv, 0.0)
-            acc_mix[...] += jnp.where(inside(k2), g_mix, 0.0)
-            dd = jnp.concatenate(
-                [d_den[pl.ds(first, 8), :], d_den[pl.ds(first + HALF, 8), :]], axis=1
-            )
-            score_ring[half][...] = (d_weight + dd) * gate_rows[new]
+                if conv:
+                    g_conv += mm_nt(window(slot, c, n), relu_ring[half][both, :])
+                if relu:
+                    h = [hid[old, F * j : F * j + F, :] for j in (2 * n, 2 * n + 1)]
+                    d2 = [second_ring[half][F * j : F * j + F, :] for j in (2 * n, 2 * n + 1)]
+                    for j in range(2):
+                        dh = mm(mix_b, d2[j]).astype(BF)
+                        at = F * (2 * n + j)
+                        relu_ring[half][at : at + F, :] = jnp.where(
+                            h[j] > 0, dh, jnp.zeros_like(dh)
+                        )
+                    g_mix += mm_nt(jnp.concatenate(h, axis=1), jnp.concatenate(d2, axis=1))
+            if second:
+                second_back(bound(k1), half, inside(k1))
+            if weight:
+                first, dn = cut(new)
+                hi, lo = split2(spread(dn[:, :F]))
+                dw = mm(jnp.concatenate([hi, lo], axis=0), feat[new])
+                dw = jnp.concatenate(
+                    [dw[:8, :R] + dw[16:24, :R], dw[8:16, R:] + dw[24:, R:]], axis=1
+                )
+                dd = jnp.concatenate(
+                    [d_den[pl.ds(first, 8), :], d_den[pl.ds(first + HALF, 8), :]], axis=1
+                )
+                score_ring[half][...] = (dw + dd) * gate_rows[new]
+                turned_ring[half][...] = jnp.concatenate([0.5 * dn, zeros(112, 128)], axis=0).T[:F]
+            if conv:
+                acc_conv[...] += jnp.where(inside(k3), g_conv, 0.0)
+            if relu:
+                acc_mix[...] += jnp.where(inside(k2), g_mix, 0.0)
+
+    backward_step(0, (0,))
+    backward_step(1, (0, 1))
+    backward_step(2, (0, 1, 2))
+
+    @pl.loop(3, steps)
+    def _(i):
+        backward_step(i, (0, 1, 2, 3))
+
+    backward_step(steps, (1, 2, 3))
+    backward_step(steps + 1, (2, 3))
+    backward_step(steps + 2, (3,))
 
     turned = acc_conv[...]
     g_conv = turned[0:24, :F] + turned[8:32, F:]
@@ -275,8 +323,11 @@
     g_query = jnp.sum(ones_f, axis=0, keepdims=True)[:, :F]
     rest = jnp.concatenate([g_conv, g_bias, g_query, zeros(6, F)], axis=0)
     gm = acc_mix[...]
-    grads[0:32, :] = jnp.concatenate([gm[:32], gm[32:]], axis=1)
-    grads[32:48, :] = jnp.concatenate([rest[:16], rest[16:]], axis=1)
+    packed = jnp.concatenate(
+        [jnp.concatenate([v[:n], v[n:]], axis=1) for v, n in ((gm, 32), (rest, 16))], axis=0
+    )
+    for n in range(GROUP):
+        grads[n] = packed
 
 
 def run_kernel(dev, counts, reads, starts, x, conv_w, bias, mix, query, cot, interpret=False):
@@ -287,7 +338,7 @@
         pooling_kernel,
         out_shape=(
             jax.ShapeDtypeStruct((F, SITES), F32),
-            jax.ShapeDtypeStruct((48, 128), F32),
+            jax.ShapeDtypeStruct((GROUP, 48, 128), F32),
         ),
         in_specs=[smem] * 4 + [pl.BlockSpec(memory_space=pl.ANY)] + [vmem] * 5,
         out_specs=(vmem, vmem),
@@ -299,16 +350,6 @@
             pltpu.VMEM((SPARE + 1, 8, 2 * R), F32),
             pltpu.VMEM((SPARE + 1, 8, 2 * R), F32),
             pltpu.VMEM((F, R), F32),
-            pltpu.VMEM(big[1:], BF),
-            pltpu.VMEM(big[1:], BF),
-            pltpu.VMEM(big[1:], BF),
-            pltpu.VMEM(big[1:], BF),
-            pltpu.VMEM((8, 2 * R), F32),
-            pltpu.VMEM((8, 2 * R), F32),
-            pltpu.VMEM(big[1:], BF),
-            pltpu.VMEM(big[1:], BF),
-            pltpu.VMEM(big[1:], BF),
-            pltpu.VMEM(big[1:], BF),
             pltpu.VMEM((WIN, F), F32),
             pltpu.VMEM((WIN, 128), F32),
             pltpu.VMEM((WIN, 128), F32),
@@ -317,7 +358,10 @@
             pltpu.VMEM((48, 128), F32),
             pltpu.VMEM((F, R), F32),
             pltpu.SemaphoreType.DMA((OWN,)),
-        ],
+        ]
+        + [pltpu.VMEM(big[1:], BF)] * (4 * STEP)
+        + [pltpu.VMEM((8, 2 * R), F32)] * STEP
+        + [pltpu.VMEM((F, 128), F32)] * STEP,
         compiler_params=pltpu.CompilerParams(vmem_limit_bytes=60 * 2**20),
         interpret=interpret,
     )(dev, counts, reads, starts, x, conv_w, bias, mix, query, cot)
@@ -334,8 +378,9 @@
         conv_weight.reshape(3 * CH, F), conv_bias.reshape(1, F), mix_weight,
         pool_query.reshape(1, F), site_cotangent[0, 0],
     )
-    for axes, size in ((("x", "core"), 8), (("z_low", "rep"), 8), ("z_high", 8)):
-        every = jnp.broadcast_to(grads, (size, *grads.shape))
+    grads = jnp.sum(lax.all_to_all(grads, ("x", "core"), 0, 0), axis=0)
+    for axes in (("z_low", "rep"), "z_high"):
+        every = jnp.broadcast_to(grads, (8, *grads.shape))
         grads = jnp.sum(lax.all_to_all(every, axes, 0, 0), axis=0)
     g_mix = jnp.concatenate([grads[:32, :F], grads[:32, F:]], axis=0)
     rest = jnp.concatenate([grads[32:, :F], grads[32:, F:]], axis=0)

time: 107 us -> 95.9 us (0.90)
  blocking collectives: 85.1 us -> 78.1 us
  Pallas kernels: 18.5 us -> 14.8 us
    all_to_all x3 -> x2, blocking collectives: 85.1 us -> 38.1 us  [on_device(): grads = jnp.sum(lax.all_to_all(every, axes, 0, 0), axis=0)]
    all_to_all x0 -> x1, blocking collectives: none -> 40 us  [on_device(): grads = jnp.sum(lax.all_to_all(grads, ('x', 'core'), 0, 0), axis=0)]
    pallas_call x1, Pallas kernels: 18.5 us -> 14.8 us  [run_kernel(): pl.pallas_call(pooling_kernel, out_shape=(jax.ShapeDtypeStruct((F, SITES)...]
where the time goes in v3:
time: 95.9 us; the launch traced here: 95.6 us
  blocking collectives  78.1 us (81%)
  Pallas kernels  14.8 us (15%)
  other arithmetic  1.27 us (1%)
    all_to_all x1, blocking collectives, on_device(): grads = jnp.sum(lax.all_to_all(grads, ('x', 'core'), 0, 0), axis=0)  40 us
    all_to_all x2, blocking collectives, on_device(): grads = jnp.sum(lax.all_to_all(every, axes, 0, 0), axis=0)  38.1 us
    pallas_call x1, Pallas kernels, run_kernel(): pl.pallas_call(pooling_kernel, out_shape=(jax.ShapeDtypeStruct((F, SITES)...  14.8 us

profile of v3, /device:TPU:2, one launch (start us, length us, event | category | flops | bytes accessed | tf_op | source)
XLA Modules:
  0.0 95.6 jit_solution(11131954485891125184)
XLA Ops:
  0.6 14.8 %shard_map.128 = (f32[64,1024]{1,0:T(8,128)}, f32[8,48,128]{2,1,0:T(8,128)}) custom-call(s32[1]{0:T(128)} %bitcast.dev, s32[1,128]{1,0:T(1,128)} %counts.1, s32[1,512]{1,0:T(1,128)} %reads.1, s32[1,512]{1,0:T(1,128)} %starts.1, bf16[1,4,221,8,128]{4,3,2,1,0:T(8,128)(2,1)} %x_hbm.1, bf16[24,64]{1,0:T(8,128)(2,1)} %bitcast.13, f32[1,64]{1,0:T(1,128)} %bitcast.14, ...), custom_call_target="tpu_custom_call" | custom-call | tf_op jit(solution)/shard_map/pallas_call | solution.py:337
  15.4 40.0 %all_to_all.15 = f32[8,48,128]{2,1,0:T(8,128)S(1)} all-to-all(f32[8,48,128]{2,1,0:T(8,128)} %get-tuple-element.8), channel_id=1, replica_groups=mesh['z_high'=8,'z_low'=2,'x'=4,'core'=2,'rep'=4] {'x','core'}, dimensions={0} | all-to-all | bytes 393216 | tf_op jit(solution)/shard_map/all_to_all | solution.py:381
  55.5 9.3 %all_to_all.16 = f32[8,48,128]{2,1,0:T(8,128)S(1)} all-to-all(f32[8,48,128]{2,1,0:T(8,128)S(1)} %broadcast_in_dim.10), channel_id=1, replica_groups=mesh['z_high'=8,'z_low'=2,'x'=4,'core'=2,'rep'=4] {'z_low','rep'}, dimensions={0} | all-to-all | bytes 393216 | tf_op jit(solution)/shard_map/all_to_all | solution.py:384
  64.9 28.8 %all_to_all.17 = f32[8,48,128]{2,1,0:T(8,128)S(1)} all-to-all(f32[8,48,128]{2,1,0:T(8,128)S(1)} %broadcast_in_dim.11), channel_id=1, replica_groups=mesh['z_high'=8,'z_low'=2,'x'=4,'core'=2,'rep'=4] {'z_high'}, dimensions={0} | all-to-all | bytes 393216 | tf_op jit(solution)/shard_map/all_to_all | solution.py:384
  93.6 0.6 slice_bitcast_fusion
  94.2 0.1 fusion.2
  94.3 0.1 fusion.1
  94.4 0.6 fusion
  95.0 0.6 pad_maximum_fusion
  (5 shorter events, 0.1 us)

commit v4 on v3

--- a/solution.py
+++ b/solution.py
@@ -56,10 +56,10 @@
 
 
 def pooling_kernel(
-    dev, counts, reads, starts, x_hbm, conv_w, bias, mix, query, cot,
-    pooled, grads,
+    dev, counts, reads, starts, x_hbm, conv_w, bias, mix, query, cot_hbm,
+    pooled_hbm, grads,
     x, hid, feat, slope, weight_rows, gate_rows, query_rows,
-    w_num, w_den, d_num, d_den, acc_mix, acc_conv, acc_query, sems, *rings,
+    w_num, w_den, d_num, d_den, acc_mix, acc_conv, acc_query, cot, pooled, sems, *rings,
 ):
     me = dev[0]
     count = counts[0, me]
@@ -72,8 +72,11 @@
         pltpu.make_async_copy(x_hbm.at[0, s], x.at[s, pl.ds(1, POS)], sems.at[s])
         for s in range(OWN)
     ]
+    cot_copy = pltpu.make_async_copy(cot_hbm, cot, sems.at[OWN])
+    pooled_copy = pltpu.make_async_copy(pooled, pooled_hbm, sems.at[OWN + 1])
     for copy in copies:
         copy.start()
+    cot_copy.start()
     for s in range(OWN):
         x[s, 0] = jnp.zeros((CH, R), BF)
         x[s, POS + 1 :] = jnp.zeros((XPOS - POS - 1, CH, R), BF)
@@ -118,8 +121,7 @@
 
     w_num[...] = jnp.zeros(w_num.shape, F32)
     w_den[...] = jnp.zeros(w_den.shape, F32)
-    for copy in copies:
-        copy.wait()
+    copies[0].wait()
 
     def first_dots(k, half, i):
         slot, c = place(jnp.minimum(k, SPARE - 1))
@@ -129,8 +131,12 @@
         hid[k, rows, :] = relu
         hid_ring[half][rows, :] = relu
 
-    def second_dots(half):
-        return [mm(mix_t, hid_ring[half][F * j : F * j + F, :]) for j in range(GROUP)]
+    def second_dot(half, j):
+        return mm(mix_t, hid_ring[half][F * j : F * j + F, :])
+
+    def score_dot(half, n):
+        rows = slice(128 * n, 128 * n + 128)
+        return mm(query_lhs[:, rows], feat_ring[half][rows, :])
 
     def second_rest(k, dots):
         for j, h in enumerate(dots):
@@ -141,9 +147,8 @@
             feat[k, rows, :] = f.astype(BF)
             slope[k, rows, :] = (a + f * (1.0 - t)).astype(BF)
 
-    def score_stage(k, half):
+    def score_stage(k, score):
         slot, c = place(k)
-        score = mm(query_lhs, feat_ring[half][...])
         score = score[:8] + score[8:]
         opening = 0.5 + 0.5 * jnp.tanh(score)
         read = jnp.where(lane8 < R, lane8, lane8 - R)
@@ -184,31 +189,49 @@
         mid = [jnp.clip(STEP * (i - 1) + n, 0, SPARE) for n in chunks]
         old = [bound(STEP * (i - 2) + n) for n in chunks]
         nums = [jnp.zeros((16, 128), F32)] * STEP
-        dots, weights = {}, {}
-        if second:
-            dots[0] = second_dots(0)
-        if pool:
-            weights = {n: score_stage(old[n], n) for n in chunks}
-        for n in chunks:
+        scores = [jnp.zeros((16, 2 * R), F32)] * STEP
+        weights, dots = {}, [[] for _ in chunks]
+
+        def mix_chunk(n, scored=()):
+            for j in range(GROUP):
+                if second:
+                    dots[n].append(second_dot(n, j))
+                if pool and j % 2:
+                    for p in scored:
+                        scores[p] += score_dot(p, j // 2)
+            if pool:
+                for p in scored:
+                    weights[p] = score_stage(old[p], scores[p])
             if second:
-                if n + 1 < STEP:
-                    dots[n + 1] = second_dots(n + 1)
-                second_rest(mid[n], dots.pop(n))
-            todo = (2 * n - 2, 2 * n - 1) if pool and n in (1, 2) else ()
+                second_rest(mid[n], dots[n])
+
+        def convolve_chunk(n, pooled=()):
             for m in range(GROUP // 2):
                 if first:
                     first_dots(new[n], n, m)
-                if m % 2:
-                    for t in todo:
-                        nums[t] = pool_dot(t, weights[t][0], nums[t], m // 2)
-            for t in todo:
-                pool_rest(old[t], weights[t][1], nums[t], inside(STEP * (i - 2) + t))
+                if pool:
+                    for p in pooled[m // 2 : m // 2 + 1]:
+                        nums[p] = pool_dot(p, weights[p][0], nums[p], m % 2)
+            if pool:
+                for p in pooled:
+                    pool_rest(old[p], weights[p][1], nums[p], inside(STEP * (i - 2) + p))
+
+        mix_chunk(0, (0, 1))
+        mix_chunk(1, (2, 3))
+        convolve_chunk(0, (0, 1))
+        mix_chunk(2)
+        convolve_chunk(1, (2, 3))
+        mix_chunk(3)
+        convolve_chunk(2)
+        convolve_chunk(3)
         if second:
             for n in chunks:
                 feat_ring[n][...] = feat[mid[n]]
 
     forward_step(0, (0,))
     forward_step(1, (0, 1))
+    for copy in copies[1:]:
+        copy.wait()
 
     @pl.loop(2, steps)
     def _(i):
@@ -217,6 +240,7 @@
     forward_step(steps, (1, 2))
     forward_step(steps + 1, (2,))
 
+    cot_copy.wait()
     d_num[SITES:, :] = jnp.zeros((WIN - SITES, 128), F32)
     d_den[SITES:, :] = jnp.zeros((WIN - SITES, 128), F32)
     for i in range(SITES // 128):
@@ -231,6 +255,8 @@
         d_num[here, :] = dn
         inner = jnp.sum(dn[:, :F] * num, axis=1, keepdims=True)
         d_den[here, :] = jnp.where(den > 1.0, -(jnp.broadcast_to(inner, (128, 128)) * inv), 0.0)
+
+    pooled_copy.start()
 
     acc_mix[...] = jnp.zeros(acc_mix.shape, F32)
     acc_conv[...] = jnp.zeros(acc_conv.shape, F32)
@@ -328,11 +354,26 @@
     )
     for n in range(GROUP):
         grads[n] = packed
+    pooled_copy.wait()
+
+
+def finish_kernel(parts, g_conv, g_bias, g_mix, g_query):
+    total = parts[0]
+    for n in range(1, GROUP):
+        total += parts[n]
+    left, right = total[:, :F], total[:, F:]
+    g_mix[:32, :] = left[:32]
+    g_mix[32:, :] = right[:32]
+    g_conv[:16, :] = left[32:]
+    g_conv[16:, :] = right[32:40]
+    g_bias[...] = right[40:41]
+    g_query[...] = right[41:42]
 
 
 def run_kernel(dev, counts, reads, starts, x, conv_w, bias, mix, query, cot, interpret=False):
     smem = pl.BlockSpec(memory_space=pltpu.SMEM)
     vmem = pl.BlockSpec(memory_space=pltpu.VMEM)
+    anywhere = pl.BlockSpec(memory_space=pl.ANY)
     big = (SPARE + 1, GROUP * F, 2 * R)
     return pl.pallas_call(
         pooling_kernel,
@@ -340,8 +381,8 @@
             jax.ShapeDtypeStruct((F, SITES), F32),
             jax.ShapeDtypeStruct((GROUP, 48, 128), F32),
         ),
-        in_specs=[smem] * 4 + [pl.BlockSpec(memory_space=pl.ANY)] + [vmem] * 5,
-        out_specs=(vmem, vmem),
+        in_specs=[smem] * 4 + [anywhere] + [vmem] * 4 + [anywhere],
+        out_specs=(anywhere, vmem),
         scratch_shapes=[
             pltpu.VMEM((OWN, XPOS, CH, R), BF),
             pltpu.VMEM(big, BF),
@@ -357,7 +398,9 @@
             pltpu.VMEM((F, F), F32),
             pltpu.VMEM((48, 128), F32),
             pltpu.VMEM((F, R), F32),
-            pltpu.SemaphoreType.DMA((OWN,)),
+            pltpu.VMEM((F, SITES), F32),
+            pltpu.VMEM((F, SITES), F32),
+            pltpu.SemaphoreType.DMA((OWN + 2,)),
         ]
         + [pltpu.VMEM(big[1:], BF)] * (4 * STEP)
         + [pltpu.VMEM((8, 2 * R), F32)] * STEP
@@ -378,13 +421,21 @@
         conv_weight.reshape(3 * CH, F), conv_bias.reshape(1, F), mix_weight,
         pool_query.reshape(1, F), site_cotangent[0, 0],
     )
-    grads = jnp.sum(lax.all_to_all(grads, ("x", "core"), 0, 0), axis=0)
+    parts = lax.all_to_all(grads, ("x", "core"), 0, 0)
     for axes in (("z_low", "rep"), "z_high"):
-        every = jnp.broadcast_to(grads, (8, *grads.shape))
-        grads = jnp.sum(lax.all_to_all(every, axes, 0, 0), axis=0)
-    g_mix = jnp.concatenate([grads[:32, :F], grads[:32, F:]], axis=0)
-    rest = jnp.concatenate([grads[32:, :F], grads[32:, F:]], axis=0)
-    return (pooled[None, None], rest[:24].reshape(3, CH, F), rest[24], g_mix, rest[25])
+        total = jnp.sum(parts, axis=0)
+        parts = lax.all_to_all(jnp.broadcast_to(total, parts.shape), axes, 0, 0)
+    vmem = pl.BlockSpec(memory_space=pltpu.VMEM)
+    shapes = [(3 * CH, F), (1, F), (F, F), (1, F)]
+    g_conv, g_bias, g_mix, g_query = pl.pallas_call(
+        finish_kernel,
+        out_shape=[jax.ShapeDtypeStruct(shape, F32) for shape in shapes],
+        in_specs=[vmem],
+        out_specs=[vmem] * 4,
+    )(parts)
+    return (
+        pooled[None, None], g_conv.reshape(3, CH, F), g_bias.reshape(F), g_mix, g_query.reshape(F)
+    )
 
 
 def solution(mesh):

time: 95.9 us -> 93.6 us (0.976)
  blocking collectives: 78.1 us -> 69.4 us
  Pallas kernels: 14.8 us -> 22.7 us
  other arithmetic: 1.27 us -> 0.03 us
    all_to_all x3, blocking collectives: 78.1 us -> 69.4 us  [the longest x2 38.1 us: on_device(): parts = lax.all_to_all(jnp.broadcast_to(total, parts.shape), axes, 0, 0)]
    pallas_call x1, Pallas kernels: 14.8 us -> 21.1 us  [run_kernel(): pl.pallas_call(pooling_kernel, out_shape=(jax.ShapeDtypeStruct((F, SITES)...]
    pallas_call x0 -> x1, Pallas kernels: none -> 1.63 us  [on_device(): pl.pallas_call(finish_kernel, out_shape=[jax.ShapeDtypeStruct(shape, F32)...]
where the time goes in v4:
time: 93.6 us; the launch traced here: 92.9 us
  blocking collectives  69.4 us (74%)
  Pallas kernels  22.7 us (24%)
    all_to_all x2, blocking collectives, on_device(): parts = lax.all_to_all(jnp.broadcast_to(total, parts.shape), axes, 0, 0)  38.1 us
    all_to_all x1, blocking collectives, on_device(): parts = lax.all_to_all(grads, ('x', 'core'), 0, 0)  31.3 us
    pallas_call x1, Pallas kernels, run_kernel(): pl.pallas_call(pooling_kernel, out_shape=(jax.ShapeDtypeStruct((F, SITES)...  21.1 us

profile of v4, /device:TPU:2, one launch (start us, length us, event | category | flops | bytes accessed | tf_op | source)
XLA Modules:
  0.0 92.9 jit_solution(2171284948380681839)
XLA Ops:
  0.6 21.1 %shard_map.128 = (f32[64,1024]{1,0:T(8,128)}, f32[8,48,128]{2,1,0:T(8,128)}) custom-call(s32[1]{0:T(128)} %bitcast.dev, s32[1,128]{1,0:T(1,128)} %counts.1, s32[1,512]{1,0:T(1,128)} %reads.1, s32[1,512]{1,0:T(1,128)} %starts.1, bf16[1,4,221,8,128]{4,3,2,1,0:T(8,128)(2,1)} %x_hbm.1, bf16[24,64]{1,0:T(8,128)(2,1)} %bitcast.10, f32[1,64]{1,0:T(1,128)} %bitcast.11, ...), custom_call_target="tpu_custom_call" | custom-call | tf_op jit(solution)/shard_map/pallas_call | solution.py:378
  21.7 31.3 %all_to_all.15 = f32[8,48,128]{2,1,0:T(8,128)S(1)} all-to-all(f32[8,48,128]{2,1,0:T(8,128)} %get-tuple-element.12), channel_id=1, replica_groups=mesh['z_high'=8,'z_low'=2,'x'=4,'core'=2,'rep'=4] {'x','core'}, dimensions={0} | all-to-all | bytes 393216 | tf_op jit(solution)/shard_map/all_to_all | solution.py:424
  53.1 9.3 %all_to_all.16 = f32[8,48,128]{2,1,0:T(8,128)S(1)} all-to-all(f32[8,48,128]{2,1,0:T(8,128)S(1)} %broadcast_in_dim.10), channel_id=1, replica_groups=mesh['z_high'=8,'z_low'=2,'x'=4,'core'=2,'rep'=4] {'z_low','rep'}, dimensions={0} | all-to-all | bytes 393216 | tf_op jit(solution)/shard_map/all_to_all | solution.py:427
  62.4 28.8 %all_to_all.17.parts = f32[8,48,128]{2,1,0:T(8,128)} all-to-all(f32[8,48,128]{2,1,0:T(8,128)S(1)} %broadcast_in_dim.11), channel_id=1, replica_groups=mesh['z_high'=8,'z_low'=2,'x'=4,'core'=2,'rep'=4] {'z_high'}, dimensions={0} | all-to-all | bytes 393216 | tf_op jit(solution)/shard_map/all_to_all | solution.py:427
  91.2 1.6 %shard_map.129 = (f32[24,64]{1,0:T(8,128)}, f32[1,64]{1,0:T(1,128)}, f32[64,64]{1,0:T(8,128)}, f32[1,64]{1,0:T(1,128)}) custom-call(f32[8,48,128]{2,1,0:T(8,128)} %all_to_all.17.parts), custom_call_target="tpu_custom_call" | custom-call | tf_op jit(solution)/shard_map/pallas_call | solution.py:430
  (4 shorter events, 0.1 us)
